TPU v7x, 32 devices: a whole 2x2x4 slice. The times are simulated.
32 devices in a mesh: groups: 2 (over y), pool: 8 (over z, x), tp: 2 (over core).
Axes of the slice: x: 2, y: 2, z: 4, core: 2. Of those that a mesh axis runs over, the one named last changes fastest.
Arguments:
- x_pre: bfloat16 [24576, 7168], P(('groups', 'pool'), 'tp'), parts along dimension 0, may hold values from -6 to 6
- x_dec: bfloat16 [224, 2, 7168], P(('groups', 'pool'), None, 'tp'), parts along dimension 0, may hold values from -6 to 6
- q_dec: bfloat16 [224, 2, 24576], P(('groups', 'pool'), None, 'tp'), parts along dimension 0, may hold values from -5 to 5
- kv_weight: bfloat16 [7168, 576], P('tp'), may hold values from -0.0625 to 0.0625
- kv_gain: float32 [512], replicated, may hold values from 0.1 to 1.9
- up_key: bfloat16 [128, 128, 512], P('tp'), may hold values from -0.5 to 0.5
- up_value: bfloat16 [128, 512, 128], P('tp'), may hold values from -0.25 to 0.25
- out_weight: bfloat16 [16384, 7168], P('tp', 'pool'), may hold values from -0.046875 to 0.046875
- old_cache: bfloat16 [96, 384, 576], P(('groups', 'pool')), parts along dimension 0, may hold values from -9 to 9
- old_lens: int32 [96], P(('groups', 'pool')), parts along dimension 0, may hold values from 1 to 384, 9216 in all
- prompt_lens: int32 [16, 8], P('groups'), parts along dimension 0, may hold values from 1 to 384, 1536 in all within a row
- owners: int32 [16, 8], P('groups'), parts along dimension 0, may hold values from 0 to 7, each once within a row
Outputs:
- attn_out: bfloat16 [448, 7168], P(('groups', 'tp'), 'pool'), parts along dimension 0
There are 2 independent parts, one for each index of `groups`. A program takes and returns all parts, laid end to end along the dimension named above; an argument that names none is the same for every part. Nothing has to cross between parts.
Inputs may be any that keep to these rules, and one draw needn't show every extreme that they name: `old_lens`: the lengths sum to 9216 and the largest is exactly 384. `prompt_lens`: each row sums to 1536 and its largest entry is exactly 384. `owners`: each row is a permutation of 0 to 7, so every pool index owns exactly one prompt of every source.
All inputs are finite; a program needn't handle non-finite values. No bound on the sum of `old_lens` on one device may be relied on, other than what follows from the above.
Results may differ from a plain program's by a relative error of at most 0.0083.
Values may be sent and summed in bfloat16 or wider, within the bound.
A program may use at most 128 MiB of HBM per device.

v0:
```python
import math

import jax
import jax.numpy as jnp
from jax import lax
from jax.sharding import PartitionSpec as P

ROPE = 64
NOPE = 128


def normalize(raw_rows, kv_gain):
    lat_width = kv_gain.shape[0]
    latent = raw_rows[..., :lat_width]
    factor = lax.rsqrt(jnp.mean(latent * latent, axis=-1, keepdims=True) + 1e-06)
    return jnp.concatenate([latent * factor * kv_gain, raw_rows[..., lat_width:]], axis=-1).astype(
        jnp.bfloat16
    )


def slot_rows(latent, starts, counts, amount):
    offsets = jnp.arange(amount, dtype=jnp.int32)
    positions = jnp.clip(starts[:, None] + offsets[None, :], 0, latent.shape[0] - 1)
    picked = jnp.take(latent, positions, axis=0)
    keep_mask = (offsets[None, :] < counts[:, None])[:, :, None]
    return jnp.where(keep_mask, picked, jnp.zeros_like(picked))


def attend(cache_rows, lengths, queries, own_keys, up_value, scaling):
    lat_width = up_value.shape[1]
    scores = (
        jnp.einsum("rihc,rlc->rihl", queries, cache_rows, preferred_element_type=jnp.float32)
        * scaling
    )
    places = jnp.arange(cache_rows.shape[1], dtype=jnp.int32)
    inside = places[None, :] < lengths[:, None]
    scores = jnp.where(inside[:, None, None, :], scores, -jnp.inf)
    recent = (
        jnp.einsum("rihc,rjc->rihj", queries, own_keys, preferred_element_type=jnp.float32)
        * scaling
    )
    positions = jnp.arange(own_keys.shape[1], dtype=jnp.int32)
    causal = positions[:, None] >= positions[None, :]
    recent = jnp.where(causal[None, :, None, :], recent, -jnp.inf)
    highest = jnp.maximum(jnp.max(scores, axis=-1), jnp.max(recent, axis=-1))[..., None]
    far_terms = jnp.exp(scores - highest)
    near_terms = jnp.exp(recent - highest)
    totals = jnp.sum(far_terms, axis=-1, keepdims=True) + jnp.sum(
        near_terms, axis=-1, keepdims=True
    )
    far_weights = (far_terms / totals).astype(jnp.bfloat16)
    near_weights = (near_terms / totals).astype(jnp.bfloat16)
    combined = jnp.einsum(
        "rihl,rlc->rihc",
        far_weights,
        cache_rows[..., :lat_width],
        preferred_element_type=jnp.float32,
    )
    combined = combined + jnp.einsum(
        "rihj,rjc->rihc",
        near_weights,
        own_keys[..., :lat_width],
        preferred_element_type=jnp.float32,
    )
    combined = combined.astype(jnp.bfloat16)
    per_head = jnp.einsum(
        "rihc,hcv->rihv", combined, up_value, preferred_element_type=jnp.float32
    ).astype(jnp.bfloat16)
    return per_head.reshape(cache_rows.shape[0] * own_keys.shape[1], -1)


def body(
    x_pre,
    x_dec,
    q_dec,
    kv_weight,
    kv_gain,
    up_key,
    up_value,
    out_weight,
    old_cache,
    old_lens,
    prompt_lens,
    owners,
):
    pool_size = lax.axis_size("pool")
    own_pool = lax.axis_index("pool")
    prompt_rows = x_pre.shape[0]
    capacity = 2 * prompt_rows // pool_size
    requests = x_dec.shape[0]
    model_part = x_pre.shape[1]
    pre_part = jnp.dot(x_pre, kv_weight, preferred_element_type=jnp.float32)
    dec_part = jnp.dot(
        x_dec.reshape(requests * 2, model_part), kv_weight, preferred_element_type=jnp.float32
    )
    my_lengths = lax.dynamic_index_in_dim(prompt_lens, own_pool, 0, keepdims=False)
    my_owners = lax.dynamic_index_in_dim(owners, own_pool, 0, keepdims=False)
    targets = jnp.arange(pool_size, dtype=jnp.int32)
    chosen = my_owners[:, None] == targets[None, :]
    begins = jnp.cumsum(my_lengths) - my_lengths
    send_start = jnp.sum(jnp.where(chosen, begins[:, None], 0), axis=0)
    send_count = jnp.sum(jnp.where(chosen, my_lengths[:, None], 0), axis=0)
    arrived_len = jnp.sum(jnp.where(owners == own_pool, prompt_lens, 0), axis=1)
    pre_sum, dec_sum = lax.psum((pre_part, dec_part), "tp")
    outgoing = slot_rows(normalize(pre_sum, kv_gain), send_start, send_count, capacity)
    new_cache = lax.all_to_all(outgoing, "pool", split_axis=0, concat_axis=0, tiled=True)
    dec_keys = normalize(dec_sum, kv_gain).reshape(requests, 2, -1)
    heads_here = up_key.shape[0]
    query_rows = q_dec.reshape(requests, 2, heads_here, NOPE + ROPE)
    absorbed = jnp.einsum(
        "rihn,hnc->rihc", query_rows[..., :NOPE], up_key, preferred_element_type=jnp.float32
    )
    full_query = jnp.concatenate([absorbed.astype(jnp.bfloat16), query_rows[..., NOPE:]], axis=-1)
    scaling = 1.0 / math.sqrt(NOPE + ROPE)
    fresh = attend(
        new_cache, arrived_len, full_query[:pool_size], dec_keys[:pool_size], up_value, scaling
    )
    earlier = attend(
        old_cache, old_lens, full_query[pool_size:], dec_keys[pool_size:], up_value, scaling
    )
    head_rows = jnp.concatenate([fresh, earlier], axis=0)
    partial_out = jnp.dot(
        lax.all_gather(head_rows, "pool", axis=0, tiled=True),
        out_weight,
        preferred_element_type=jnp.float32,
    )
    return lax.psum_scatter(partial_out, "tp", scatter_dimension=0, tiled=True).astype(jnp.bfloat16)


def solution(mesh):
    placed = (
        P(("groups", "pool"), "tp"),
        P(("groups", "pool"), None, "tp"),
        P(("groups", "pool"), None, "tp"),
        P("tp", None),
        P(),
        P("tp", None, None),
        P("tp", None, None),
        P("tp", "pool"),
        P(("groups", "pool"), None, None),
        P(("groups", "pool")),
        P("groups", None),
        P("groups", None),
    )
    return jax.shard_map(
        body, mesh=mesh, in_specs=placed, out_specs=P(("groups", "tp"), "pool"), check_vma=False
    )
```

profile of v0, /device:TPU:0, one launch (start us, length us, event | category | flops | bytes accessed | tf_op | source)
XLA Modules:
  0.0 273.3 jit_solution(5753768217182138240)
XLA Ops:
  6.5 11.8 %fusion.81 = f32[1536,576]{0,1:T(8,128)} fusion(bf16[1536,3584]{1,0:T(8,128)(2,1)} %param.12, bf16[3584,576]{0,1:T(8,128)(2,1)} %param.15), kind=kOutput, calls=%fused_computation.107 | convolution fusion | flops 6341787648 | bytes 18677760 | tf_op jit(solution)/shard_map/dot_general | solution.py:92
  18.4 0.6 copy-done.4
  19.3 0.7 dynamic-slice_bitcast_fusion
  20.2 25.0 %all-reduce.2.cloned.1.call-done = f32[1536,576]{0,1:T(8,128)} async-done(((f32[1536,576]{0,1:T(8,128)}), f32[1536,576]{0,1:T(8,128)}) %all-reduce.2.cloned.1.call-update) | async-done | bytes 3538960 | tf_op jit(solution)/shard_map/psum | solution.py:104
  45.2 2.3 multiply_reduce_fusion
  47.6 1.0 slice.113
  48.9 1.3 pad_maximum_fusion
  50.3 2.7 %copy.31 = bf16[1536,576]{1,0:T(8,128)(2,1)S(1)} copy(bf16[1536,576]{0,1:T(8,128)(2,1)} %pad_maximum_fusion) | data formatting | bytes 3538944 | tf_op jit(solution)/shard_map/concatenate | solution.py:16
  53.0 13.5 %gather_fusion = bf16[3072,576]{1,0:T(8,128)(2,1)} fusion(bf16[1536,576]{1,0:T(8,128)(2,1)S(1)} %copy.31, s32[3072]{0:T(1024)S(1)} %broadcast_clamp_fusion), kind=kCustom, calls=%fused_computation | custom fusion | bytes 7090176 | tf_op jit(solution)/shard_map/jit(_take)/gather | solution.py:24
  66.5 4.6 %copy.33 = bf16[8,384,576]{1,2,0:T(8,128)(2,1)S(1)} copy(bf16[8,384,576]{2,1,0:T(8,128)(2,1)} %bitcast.116) | data formatting | bytes 7077888 | tf_op jit(solution)/shard_map/jit(_take)/gather | solution.py:24
  71.1 2.3 select_select_fusion
  73.4 5.9 %all-to-all-start = ((bf16[8,384,576]{1,2,0:T(8,128)(2,1)}), bf16[8,384,576]{1,2,0:T(8,128)(2,1)}, u32[]{:S(2)}, u32[]{:S(2)}) async-start(bf16[8,384,576]{1,2,0:T(8,128)(2,1)} %select_select_fusion), calls=%async_computation | async-start | bytes 7077888 | tf_op jit(solution)/shard_map/all_to_all | solution.py:106
  79.5 3.5 %fusion.82 = f32[28,576]{1,0:T(8,128)S(1)} fusion(bf16[28,3584]{1,0:T(8,128)(2,1)S(1)} %reshape.216, bf16[3584,576]{0,1:T(8,128)(2,1)} %param.15), kind=kOutput, calls=%fused_computation.108 | convolution fusion | flops 115605504 | bytes 4393984 | tf_op jit(solution)/shard_map/dot_general | solution.py:93
  83.0 3.7 %psum.15 = f32[28,576]{1,0:T(8,128)S(1)} all-reduce(f32[28,576]{1,0:T(8,128)S(1)} %fusion.82), channel_id=1, replica_groups=mesh['groups'=2,'pool'=8,'tp'=2] {'tp'}, use_global_device_ids=true, to_apply=%region_7.8 | all-reduce | flops 16128 | bytes 129024 | tf_op jit(solution)/shard_map/psum | solution.py:104
  87.0 1.0 reshape.213
  88.6 4.8 %convert_bitcast_fusion = bf16[14,2,64,512]{3,0,1,2:T(8,128)(2,1)S(1)} fusion(bf16[64,128,512]{2,1,0:T(8,128)(2,1)} %param.17, bf16[14,2,64,128]{3,2,1,0:T(8,128)(2,1)S(1)} %slice.68), kind=kOutput, calls=%fused_computation.22 | convolution fusion | flops 235798528 | bytes 10682368 | tf_op jit(solution)/shard_map/rihn,hnc->rihc/dot_general | solution.py:110
  95.2 0.9 fusion.77
  97.0 0.9 add_convert_fusion.1
  98.0 1.0 slice-done.1
  99.0 1.8 fusion.34
  101.4 0.7 fusion.80
  102.2 56.9 %all-to-all-done = bf16[8,384,576]{1,2,0:T(8,128)(2,1)} async-done(((bf16[8,384,576]{1,2,0:T(8,128)(2,1)}), bf16[8,384,576]{1,2,0:T(8,128)(2,1)}, u32[]{:S(2)}, u32[]{:S(2)}) %all-to-all-start) | async-done | bytes 3538976 | tf_op jit(solution)/shard_map/all_to_all | solution.py:106
  159.0 3.3 %fusion.79 = (f32[8,2,64]{2,1,0:T(2,128)S(1)}, f32[8,2,64,384]{3,2,1,0:T(8,128)S(1)}) fusion(bf16[8,384,576]{1,2,0:T(8,128)(2,1)} %all-to-all-done, bf16[8,2,64,576]{3,0,1,2:T(8,128)(2,1)S(1)} %fusion.27, pred[8,384]{1,0:T(8,128)(4,1)S(1)} %iota_compare_fusion.2), kind=kOutput, calls=%fused_computation.105 | convolution fusion | flops 454163456 | bytes 6298624 | tf_op jit(solution)/shard_map/rihc,rlc->rihl/dot_general | solution.py:32
  162.4 0.6 fusion.26
  163.5 3.3 %add_convert_fusion = bf16[8,2,64,512]{3,2,1,0:T(8,128)(2,1)S(1)} fusion(f32[8,2,64,512]{3,2,1,0:T(8,128)S(1)} %fusion.62, bf16[8,384,576]{1,2,0:T(8,128)(2,1)} %all-to-all-done, f32[8,2,64,384]{3,2,1,0:T(8,128)S(1)} %get-tuple-element.14, f32[8,2,64]{2,1,0:T(2,128)S(1)} %add.109, f32[8,2,64]{2,1,0:T(2,128)S(1)} %max.24), kind=kOutput, calls=%fused_computation.21 | convolution fusion | flops 404881408 | bytes 7872512 | tf_op jit(solution)/shard_map/rihl,rlc->rihc/dot_general | solution.py:53
  166.8 1.8 fusion.37
  168.9 0.8 maximum_bitcast_fusion
  169.8 72.5 %all-gather.3.cloned.1.call-done = bf16[8,28,8192]{2,1,0:T(8,128)(2,1)} async-done(((bf16[1,28,8192]{2,1,0:T(8,128)(2,1)}), bf16[8,28,8192]{2,1,0:T(8,128)(2,1)}) %all-gather.3.cloned.1.call-update) | async-done | bytes 3670032 | tf_op jit(solution)/shard_map/all_gather | solution.py:123
  242.3 4.9 %reshape.229 = bf16[224,8192]{1,0:T(8,128)(2,1)} reshape(bf16[8,28,8192]{2,1,0:T(8,128)(2,1)} %all-gather.3.cloned.1.call-done) | data formatting | bytes 7340032
  247.2 11.1 %fusion.83 = f32[224,896]{1,0:T(8,128)} fusion(bf16[224,8192]{1,0:T(8,128)(2,1)} %reshape.229, bf16[8192,896]{1,0:T(8,128)(2,1)} %param.19), kind=kOutput, calls=%fused_computation.109 | convolution fusion | flops 3288334336 | bytes 19152896 | tf_op jit(solution)/shard_map/dot_general | solution.py:122
  258.3 6.7 %reduce-scatter.2.cloned.1.call-done = f32[112,896]{1,0:T(8,128)} async-done(((f32[224,896]{1,0:T(8,128)}), f32[112,896]{1,0:T(8,128)}) %reduce-scatter.2.cloned.1.call-update) | async-done | bytes 401424 | tf_op jit(solution)/shard_map/reduce_scatter | solution.py:127
  265.0 1.7 convert_element_type.53
  (75 shorter events, 5.9 us)
Async XLA Ops:
  6.5 38.7 %all-reduce.2.cloned.1.call-start = ((), (), s32[]{:S(2)}) async-start(), calls=%async_computation.2 | async-start | bytes 7077888 | tf_op jit(solution)/shard_map/psum | solution.py:104
  18.4 0.7 copy-start.4
  18.4 30.2 %copy-start.3 = (f32[512]{0:T(512)S(1)}, f32[512]{0:T(512)}, u32[]{:S(2)}) copy-start(f32[512]{0:T(512)} %param.16) | copy-start | bytes 6148
  45.2 3.4 %copy-start = (f32[1536,576]{0,1:T(8,128)S(1)}, f32[1536,576]{0,1:T(8,128)}, u32[]{:S(2)}) copy-start(f32[1536,576]{0,1:T(8,128)} %all-reduce.2.cloned.1.call-done) | copy-start | bytes 10616836
  73.4 6.0 %copy-start.2 = (bf16[14,2,3584]{2,1,0:T(2,128)(2,1)S(1)}, bf16[14,2,3584]{2,1,0:T(2,128)(2,1)}, u32[]{:S(2)}) copy-start(bf16[14,2,3584]{2,1,0:T(2,128)(2,1)} %param.13) | copy-start | bytes 602116
  73.4 85.6 %all-to-all-start = ((bf16[8,384,576]{1,2,0:T(8,128)(2,1)}), bf16[8,384,576]{1,2,0:T(8,128)(2,1)}, u32[]{:S(2)}, u32[]{:S(2)}) async-start(bf16[8,384,576]{1,2,0:T(8,128)(2,1)} %select_select_fusion), calls=%async_computation | async-start | bytes 7077888 | tf_op jit(solution)/shard_map/all_to_all | solution.py:106
  79.3 163.0 %all-gather.3.cloned.1.call-start = ((), (), s32[]{:S(2)}) async-start(), calls=%async_computation.4 | async-start | bytes 4718592 | tf_op jit(solution)/shard_map/all_gather | solution.py:123
  79.5 7.6 %copy-start.1 = (bf16[14,2,12288]{2,1,0:T(2,128)(2,1)S(1)}, bf16[14,2,12288]{2,1,0:T(2,128)(2,1)}, u32[]{:S(2)}) copy-start(bf16[14,2,12288]{2,1,0:T(2,128)(2,1)} %param.14) | copy-start | bytes 2064388
  93.4 0.7 copy-start.6
  93.4 1.8 copy-start.7
  95.2 2.8 %slice-start = ((s8[8388608]{0:T(1024)(128)(4,1)}), s8[4194304]{0:T(1024)(128)(4,1)S(1)}, s32[]{:S(2)}) async-start(s8[8388608]{0:T(1024)(128)(4,1)} %bitcast.112), calls=%async_computation.5 | async-start | bytes 8388608
  96.6 2.4 slice-start.1
  99.0 2.1 copy-start.5
  159.0 7.8 %slice-start.2 = ((s8[8388608]{0:T(1024)(128)(4,1)}), s8[4194304]{0:T(1024)(128)(4,1)S(1)}, s32[]{:S(2)}) async-start(s8[8388608]{0:T(1024)(128)(4,1)} %bitcast.114), calls=%async_computation.7 | async-start | bytes 8388608
  163.5 3.3 %slice-start.3 = ((s8[8388608]{0:T(1024)(128)(4,1)}), s8[4194304]{0:T(1024)(128)(4,1)S(1)}, s32[]{:S(2)}) async-start(s8[8388608]{0:T(1024)(128)(4,1)} %bitcast.114), calls=%async_computation.8 | async-start | bytes 8388608
  169.7 95.3 %reduce-scatter.2.cloned.1.call-start = ((), (), s32[]{:S(2)}) async-start(), calls=%async_computation.3 | async-start | bytes 1204224 | tf_op jit(solution)/shard_map/reduce_scatter | solution.py:127
Sparse Core Ops, SparseCore 0:
  18.5 26.6 all-reduce.1
  169.8 72.4 all-gather.2
  258.5 6.5 reduce-scatter.1
where the time goes:
time: 274 us; the launch traced here: 273 us
  waiting for transfers between devices  161 us (59%)
  matrix products  45.5 us (17%)
  local copies, waits for them, and re-layouts  32 us (12%)
  between operations  13.5 us (5%)
  other arithmetic  11.4 us (4%)
  starting transfers between devices  5.99 us (2%)
  blocking collectives  3.74 us (1%)
    all_gather x1, waiting for transfers between devices, body(): lax.all_gather(head_rows, 'pool', axis=0, tiled=True)  72.5 us
    all_to_all x1, waiting for transfers between devices, body(): lax.all_to_all(outgoing, 'pool', split_axis=0, concat_axis=0, tiled=True)  56.9 us
    psum x1, waiting for transfers between devices, body(): pre_sum, dec_sum = lax.psum((pre_part, dec_part), 'tp')  25 us
    gather x2, local copies, waits for them, and re-layouts, slot_rows(): picked = jnp.take(latent, positions, axis=0)  18 us
    dot_general x1, matrix products, body(): pre_part = jnp.dot(x_pre, kv_weight, preferred_element_type=jnp.float32)  11.8 us
    dot_general x1, matrix products, body(): jnp.dot(lax.all_gather(head_rows, 'pool', axis=0, tiled=True), out_weight...  11.1 us
    unnamed x29, local copies, waits for them, and re-layouts  7.98 us
    reduce_scatter x1, waiting for transfers between devices, body(): lax.psum_scatter(partial_out, 'tp', scatter_dimension=0, tiled=True)  6.69 us
  transfers between devices with their start and end apart: 4, of which 4 were waited for; matrix products, arithmetic and copies ran while one was open for 7% of the time, Pallas kernels for 0%

commit v1 on v0

v1 whole, which is shorter than its diff:
```python
import math

import jax
import jax.numpy as jnp
from jax import lax
from jax.sharding import PartitionSpec as P

ROPE = 64
NOPE = 128


def normalize(raw_rows, kv_gain):
    lat_width = kv_gain.shape[0]
    latent = raw_rows[..., :lat_width]
    factor = lax.rsqrt(jnp.mean(latent * latent, axis=-1, keepdims=True) + 1e-06)
    return jnp.concatenate([latent * factor * kv_gain, raw_rows[..., lat_width:]], axis=-1).astype(
        jnp.bfloat16
    )


def tp_sum(part):
    if lax.axis_size("tp") == 2:
        return part + lax.ppermute(part, "tp", [(0, 1), (1, 0)])
    return lax.psum(part, "tp")


def tp_scatter(part):
    if lax.axis_size("tp") == 2:
        half = part.shape[0] // 2
        me = lax.axis_index("tp")
        mine = lax.dynamic_slice_in_dim(part, me * half, half, 0)
        other = lax.dynamic_slice_in_dim(part, (1 - me) * half, half, 0)
        return mine + lax.ppermute(other, "tp", [(0, 1), (1, 0)])
    return lax.psum_scatter(part, "tp", scatter_dimension=0, tiled=True)


def attend(cache, inside, queries, own_keys, lat_width, scaling):
    scores = jnp.einsum("bgihc,blc->bgihl", queries, cache, preferred_element_type=jnp.float32)
    scores = jnp.where(inside[:, :, None, None, :], scores * scaling, -jnp.inf)
    recent = (
        jnp.einsum("bgihc,bgjc->bgihj", queries, own_keys, preferred_element_type=jnp.float32)
        * scaling
    )
    positions = jnp.arange(own_keys.shape[2], dtype=jnp.int32)
    causal = positions[:, None] >= positions[None, :]
    recent = jnp.where(causal[:, None, :], recent, -jnp.inf)
    highest = jnp.maximum(jnp.max(scores, axis=-1), jnp.max(recent, axis=-1))[..., None]
    far = jnp.exp(scores - highest)
    near = jnp.exp(recent - highest)
    totals = jnp.sum(far, axis=-1, keepdims=True) + jnp.sum(near, axis=-1, keepdims=True)
    combined = jnp.einsum(
        "bgihl,blc->bgihc",
        far.astype(jnp.bfloat16),
        cache[..., :lat_width],
        preferred_element_type=jnp.float32,
    )
    keys = own_keys[..., :lat_width].astype(jnp.float32)
    for j in range(own_keys.shape[2]):
        combined = combined + near[..., j : j + 1] * keys[:, :, j][:, :, None, None, :]
    return (combined / totals).astype(jnp.bfloat16)


def body(
    x_pre,
    x_dec,
    q_dec,
    kv_weight,
    kv_gain,
    up_key,
    up_value,
    out_weight,
    old_cache,
    old_lens,
    prompt_lens,
    owners,
):
    pool_size = lax.axis_size("pool")
    own_pool = lax.axis_index("pool")
    requests = x_dec.shape[0]
    model_part = x_pre.shape[1]
    heads_here = up_key.shape[0]
    lat_width = kv_gain.shape[0]
    scaling = 1.0 / math.sqrt(NOPE + ROPE)

    fresh_q = lax.all_to_all(q_dec[:pool_size], "pool", split_axis=0, concat_axis=0, tiled=True)
    fresh_x = lax.all_to_all(x_dec[:pool_size], "pool", split_axis=0, concat_axis=0, tiled=True)

    chunks = 4
    rows = x_pre.shape[0] // chunks
    pre_rows = jnp.concatenate(
        [
            normalize(
                tp_sum(
                    jnp.dot(
                        x_pre[c * rows : (c + 1) * rows],
                        kv_weight,
                        preferred_element_type=jnp.float32,
                    )
                ),
                kv_gain,
            )
            for c in range(chunks)
        ],
        axis=0,
    )
    x_rows = jnp.concatenate([fresh_x, x_dec[pool_size:]], axis=0).reshape(-1, model_part)
    dec_raw = tp_sum(jnp.dot(x_rows, kv_weight, preferred_element_type=jnp.float32))
    dec_keys = normalize(dec_raw, kv_gain).reshape(requests, 2, -1)

    my_lengths = lax.dynamic_index_in_dim(prompt_lens, own_pool, 0, keepdims=False)
    my_owners = lax.dynamic_index_in_dim(owners, own_pool, 0, keepdims=False)
    targets = jnp.arange(pool_size, dtype=jnp.int32)
    chosen = my_owners[:, None] == targets[None, :]
    begins = jnp.cumsum(my_lengths) - my_lengths
    start = jnp.sum(jnp.where(chosen, begins[:, None], 0), axis=0)
    count = jnp.sum(jnp.where(chosen, my_lengths[:, None], 0), axis=0)
    places = jnp.arange(x_pre.shape[0], dtype=jnp.int32)
    fresh_inside = (places[None] >= start[:, None]) & (places[None] < (start + count)[:, None])
    old_inside = jnp.arange(old_cache.shape[1], dtype=jnp.int32)[None] < old_lens[:, None]

    q_rows = jnp.concatenate([fresh_q, q_dec[pool_size:]], axis=0).reshape(
        requests, 2, heads_here, NOPE + ROPE
    )
    absorbed = jnp.einsum(
        "rihn,hnc->rihc", q_rows[..., :NOPE], up_key, preferred_element_type=jnp.float32
    )
    full_query = jnp.concatenate([absorbed.astype(jnp.bfloat16), q_rows[..., NOPE:]], axis=-1)
    earlier = attend(
        old_cache,
        old_inside[:, None],
        full_query[pool_size:, None],
        dec_keys[pool_size:, None],
        lat_width,
        scaling,
    )[:, 0]
    fresh = attend(
        pre_rows[None],
        fresh_inside[None],
        full_query[None, :pool_size],
        dec_keys[None, :pool_size],
        lat_width,
        scaling,
    )[0]
    combined = jnp.concatenate([fresh, earlier], axis=0)
    head_rows = (
        jnp.einsum("rihc,hcv->rihv", combined, up_value, preferred_element_type=jnp.float32)
        .astype(jnp.bfloat16)
        .reshape(requests * 2, -1)
    )
    gathered = lax.all_gather(head_rows, "pool", axis=0, tiled=True)
    partial_out = jnp.dot(gathered, out_weight, preferred_element_type=jnp.float32)
    cols = partial_out.shape[-1]
    partial_out = partial_out.reshape(pool_size, requests, 2, cols)
    partial_out = jnp.concatenate(
        [partial_out[:, :pool_size].transpose(1, 0, 2, 3), partial_out[:, pool_size:]], axis=1
    ).reshape(-1, cols)
    return tp_scatter(partial_out).astype(jnp.bfloat16)


def solution(mesh):
    placed = (
        P(("groups", "pool"), "tp"),
        P(("groups", "pool"), None, "tp"),
        P(("groups", "pool"), None, "tp"),
        P("tp", None),
        P(),
        P("tp", None, None),
        P("tp", None, None),
        P("tp", "pool"),
        P(("groups", "pool"), None, None),
        P(("groups", "pool")),
        P("groups", None),
        P("groups", None),
    )
    return jax.shard_map(
        body, mesh=mesh, in_specs=placed, out_specs=P(("groups", "tp"), "pool"), check_vma=False
    )
```

time: 274 us -> 201 us (0.73)
  waiting for transfers between devices: 161 us -> 81.5 us
  local copies, waits for them, and re-layouts: 32 us -> 14.8 us
  other arithmetic: 11.4 us -> 22.3 us
  starting transfers between devices: 5.99 us -> 15 us
  matrix products: 45.5 us -> 52.2 us
  blocking collectives: 3.74 us -> 0 us
    all_to_all x1 -> x2, waiting for transfers between devices: 56.9 us -> 5.91 us  [the longest x1 5.91 us: body(): lax.all_to_all(q_dec[:pool_size], 'pool', split_axis=0, concat_axis=0, ti...]
    psum x1 -> x0, waiting for transfers between devices: 25 us -> none  [body(): pre_sum, dec_sum = lax.psum((pre_part, dec_part), 'tp')]
    gather x2 -> x0, local copies, waits for them, and re-layouts: 18 us -> none  [slot_rows(): picked = jnp.take(latent, positions, axis=0)]
    all_to_all x1 -> x2, starting transfers between devices: 5.91 us -> 13.4 us  [the longest x1 7.25 us: body(): lax.all_to_all(x_dec[:pool_size], 'pool', split_axis=0, concat_axis=0, ti...]
    dot_general x14, matrix products: 45.5 us -> 52.2 us  [the longest x4 17.1 us: body(): jnp.dot(x_pre[c * rows:(c + 1) * rows], kv_weight, preferred_element_type...]
    reduce_scatter x1 -> x0, waiting for transfers between devices: 6.69 us -> none  [body(): lax.psum_scatter(partial_out, 'tp', scatter_dimension=0, tiled=True)]
    broadcast_in_dim x0 -> x1, other arithmetic: none -> 6.5 us  [body(): pre_rows[None]]
    add x2 -> x8, other arithmetic: 0.01 us -> 5.94 us  [the longest x5 5.92 us: tp_sum(): return part + lax.ppermute(part, 'tp', [(0, 1), (1, 0)])]
  transfers between devices with their start and end apart: 4 -> 9, of which waited for: 4 -> 4; matrix products, arithmetic and copies ran while one was open for 7% -> 22% of each run, Pallas kernels for 0% -> 0%
where the time goes in v1:
time: 201 us; the launch traced here: 200 us
  waiting for transfers between devices  81.5 us (41%)
  matrix products  52.2 us (26%)
  other arithmetic  22.3 us (11%)
  starting transfers between devices  15 us (7%)
  local copies, waits for them, and re-layouts  14.8 us (7%)
  between operations  14 us (7%)
    all_gather x1, waiting for transfers between devices, body(): gathered = lax.all_gather(head_rows, 'pool', axis=0, tiled=True)  72.6 us
    dot_general x4, matrix products, body(): jnp.dot(x_pre[c * rows:(c + 1) * rows], kv_weight, preferred_element_type...  17.1 us
    dot_general x1, matrix products, body(): jnp.dot(gathered, out_weight, preferred_element_type=jnp.float32)  10.5 us
    unnamed x25, local copies, waits for them, and re-layouts  7.84 us
    all_to_all x1, starting transfers between devices, body(): lax.all_to_all(x_dec[:pool_size], 'pool', split_axis=0, concat_axis=0, ti...  7.25 us
    dot_general x2, matrix products, attend(): jnp.einsum('bgihl,blc->bgihc', far.astype(jnp.bfloat16), cache[..., :lat_...  6.77 us
    broadcast_in_dim x1, other arithmetic, body(): pre_rows[None]  6.5 us
    all_to_all x1, starting transfers between devices, body(): lax.all_to_all(q_dec[:pool_size], 'pool', split_axis=0, concat_axis=0, ti...  6.1 us
  transfers between devices with their start and end apart: 9, of which 4 were waited for; matrix products, arithmetic and copies ran while one was open for 22% of the time, Pallas kernels for 0%

profile of v1, /device:TPU:0, one launch (start us, length us, event | category | flops | bytes accessed | tf_op | source)
XLA Modules:
  0.0 199.9 jit_solution(15793144688578731399)
XLA Ops:
  6.5 1.6 slice.138
  8.2 7.3 %all-to-all-start.1 = ((bf16[8,2,3584]{2,1,0:T(2,128)(2,1)}), bf16[8,2,3584]{2,1,0:T(2,128)(2,1)S(1)}, u32[]{:S(2)}, u32[]{:S(2)}) async-start(bf16[8,2,3584]{2,1,0:T(2,128)(2,1)} %slice.138), calls=%async_computation.1 | async-start | bytes 229376 | tf_op jit(solution)/shard_map/all_to_all | solution.py:86
  15.4 6.4 %fusion.9 = f32[384,576]{0,1:T(8,128)} fusion(bf16[3584,576]{0,1:T(8,128)(2,1)} %param.15, bf16[1536,3584]{1,0:T(8,128)(2,1)} %param.12), kind=kOutput, calls=%fused_computation.11 | convolution fusion | flops 1585446912 | bytes 7766016 | tf_op jit(solution)/shard_map/dot_general | solution.py:94
  21.8 4.2 %fusion.15 = f32[384,576]{0,1:T(8,128)S(1)} fusion(bf16[3584,576]{0,1:T(8,128)(2,1)S(1)} %copy-done.2, bf16[1536,3584]{1,0:T(8,128)(2,1)} %param.12), kind=kOutput, calls=%fused_computation.17 | convolution fusion | flops 1585446912 | bytes 7766016 | tf_op jit(solution)/shard_map/dot_general | solution.py:94
  26.9 3.2 %fusion.13 = f32[384,576]{0,1:T(8,128)} fusion(bf16[3584,576]{0,1:T(8,128)(2,1)S(1)} %copy-done.2, bf16[1536,3584]{1,0:T(8,128)(2,1)S(1)} %copy-done.9), kind=kOutput, calls=%fused_computation.15 | convolution fusion | flops 1585446912 | bytes 7766016 | tf_op jit(solution)/shard_map/dot_general | solution.py:94
  30.2 3.2 %fusion.11 = f32[384,576]{0,1:T(8,128)} fusion(bf16[3584,576]{0,1:T(8,128)(2,1)S(1)} %copy-done.2, bf16[1536,3584]{1,0:T(8,128)(2,1)S(1)} %copy-done.9), kind=kOutput, calls=%fused_computation.13 | convolution fusion | flops 1585446912 | bytes 7766016 | tf_op jit(solution)/shard_map/dot_general | solution.py:94
  33.9 1.0 slice.121
  36.8 6.1 %all-to-all-start = ((bf16[8,2,12288]{2,1,0:T(2,128)(2,1)}), bf16[8,2,12288]{2,1,0:T(2,128)(2,1)S(1)}, u32[]{:S(2)}, u32[]{:S(2)}) async-start(bf16[8,2,12288]{2,1,0:T(2,128)(2,1)} %slice.121), calls=%async_computation | async-start | bytes 786432 | tf_op jit(solution)/shard_map/all_to_all | solution.py:85
  43.5 3.5 %fusion.89 = f32[28,576]{1,0:T(8,128)S(1)} fusion(bf16[28,3584]{1,0:T(8,128)(2,1)S(1)} %reshape.306, bf16[3584,576]{0,1:T(8,128)(2,1)} %param.15), kind=kOutput, calls=%fused_computation.126 | convolution fusion | flops 115605504 | bytes 4393984 | tf_op jit(solution)/shard_map/dot_general | solution.py:107
  47.1 1.3 collective-permute-done.4
  48.8 5.9 %all-to-all-done = bf16[8,2,12288]{2,1,0:T(2,128)(2,1)S(1)} async-done(((bf16[8,2,12288]{2,1,0:T(2,128)(2,1)}), bf16[8,2,12288]{2,1,0:T(2,128)(2,1)S(1)}, u32[]{:S(2)}, u32[]{:S(2)}) %all-to-all-start) | async-done | bytes 393248 | tf_op jit(solution)/shard_map/all_to_all | solution.py:85
  54.8 0.9 pad_maximum_fusion.2
  55.6 1.0 reshape.305
  57.2 4.7 %convert_bitcast_fusion = bf16[14,2,64,512]{3,0,1,2:T(8,128)(2,1)S(1)} fusion(bf16[64,128,512]{2,1,0:T(8,128)(2,1)} %param.17, bf16[14,2,64,128]{3,2,1,0:T(8,128)(2,1)S(1)} %slice.159), kind=kOutput, calls=%fused_computation.33 | convolution fusion | flops 235798528 | bytes 10682368 | tf_op jit(solution)/shard_map/rihn,hnc->rihc/dot_general | solution.py:124
  62.5 1.6 copy-done.3
  64.0 0.9 fusion.87
  67.2 2.6 %fusion.19 = f32[6,2,64,512]{3,2,1,0:T(8,128)S(1)} fusion(bf16[6,384,576]{1,2,0:T(8,128)(2,1)} %param.20, f32[6,2,64,384]{3,2,1,0:T(8,128)S(1)} %get-tuple-element.32, f32[6,2,64]{2,1,0:T(2,128)S(1)} %max.19), kind=kOutput, calls=%fused_computation.23 | convolution fusion | flops 302579712 | bytes 5114880 | tf_op jit(solution)/shard_map/bgihl,blc->bgihc/dot_general | solution.py:51
  69.8 1.6 fusion.27
  71.5 1.5 add.116
  73.0 1.5 add.114
  74.6 1.5 add.112
  76.4 1.3 add.110
  78.3 6.5 %fusion.80 = bf16[1,1536,576]{1,2,0:T(8,128)(2,1)S(1)} fusion(bf16[384,64]{0,1:T(8,128)(2,1)S(1)} %slice.234, bf16[384,512]{0,1:T(8,128)(2,1)S(1)} %get-tuple-element.26, bf16[384,64]{0,1:T(8,128)(2,1)S(1)} %slice.235, bf16[384,512]{0,1:T(8,128)(2,1)S(1)} %get-tuple-element.25, bf16[384,64]{0,1:T(8,128)(2,1)S(1)} %slice.236, ...), kind=kLoop, calls=%fused_computation.118 | loop fusion | flops 14155776 | bytes 3538944 | tf_op jit(solution)/shard_map/broadcast_in_dim | solution.py:137
  84.8 2.7 %fusion.4 = (f32[8,2,64]{2,1,0:T(2,128)S(1)}, f32[8,2,64,1536]{3,2,1,0:T(8,128)S(1)}) fusion(pred[8,1536]{1,0:T(8,128)(4,1)S(1)} %fusion.68, bf16[384,64]{0,1:T(8,128)(2,1)S(1)} %slice.234, bf16[384,512]{0,1:T(8,128)(2,1)S(1)} %get-tuple-element.26, bf16[384,64]{0,1:T(8,128)(2,1)S(1)} %slice.235, bf16[384,512]{0,1:T(8,128)(2,1)S(1)} %get-tuple-element.25, ...), kind=kOutput, calls=%fused_computation.6 | convolution fusion | flops 1830812672 | bytes 9256960 | tf_op jit(solution)/shard_map/bgihc,blc->bgihl/dot_general | solution.py:38
  87.6 2.8 %fusion.6 = (bf16[8,2,64,1536]{3,2,1,0:T(8,128)(2,1)}, f32[8,2,64]{2,1,0:T(2,128)S(1)}) fusion(f32[8,2,64,1536]{3,2,1,0:T(8,128)S(1)} %get-tuple-element.28, f32[8,2,64]{2,1,0:T(2,128)S(1)} %max.18, pred[8,1536]{1,0:T(8,128)(4,1)S(1)} %fusion.68), kind=kLoop, calls=%fused_computation.8 | loop fusion | flops 7863296 | bytes 9457664 | tf_op jit(solution)/shard_map/convert_element_type | solution.py:53
  90.8 4.2 %divide_convert_fusion = bf16[8,2,64,512]{3,0,1,2:T(8,128)(2,1)S(1)} fusion(f32[8,2,64]{0,1,2:T(2,128)S(1)} %copy.63, f32[8,512]{1,0:T(8,128)S(1)} %get-tuple-element.37, f32[8,2,64]{0,1,2:T(2,128)S(1)} %copy.62, f32[8,512]{1,0:T(8,128)S(1)} %get-tuple-element.38, f32[8,2,64]{0,1,2:T(2,128)S(1)} %copy.61, bf16[1,1536,576]{1,2,0:T(8,128)(2,1)S(1)} %fusion.80, ...), kind=kOutput, calls=%fused_computation.32 | convolution fusion | flops 1613758464 | bytes 5996544 | tf_op jit(solution)/shard_map/bgihl,blc->bgihc/dot_general | solution.py:51
  94.9 4.6 %fusion.44 = bf16[14,2,64,128]{3,0,1,2:T(8,128)(2,1)S(1)} fusion(bf16[64,512,128]{2,1,0:T(8,128)(2,1)} %param.18, bf16[6,2,64,512]{3,0,1,2:T(8,128)(2,1)S(1)} %fusion.27, bf16[8,2,64,512]{3,0,1,2:T(8,128)(2,1)S(1)} %divide_convert_fusion), kind=kOutput, calls=%fused_computation.44 | convolution fusion | flops 238780416 | bytes 10682368 | tf_op jit(solution)/shard_map/rihc,hcv->rihv/dot_general | solution.py:146
  99.8 1.0 reshape.313
  100.9 72.6 %all-gather.3.cloned.1.call-done = bf16[8,28,8192]{2,1,0:T(8,128)(2,1)} async-done(((bf16[1,28,8192]{2,1,0:T(8,128)(2,1)}), bf16[8,28,8192]{2,1,0:T(8,128)(2,1)}) %all-gather.3.cloned.1.call-update) | async-done | bytes 3670032 | tf_op jit(solution)/shard_map/all_gather | solution.py:150
  173.5 4.9 %reshape.314 = bf16[224,8192]{1,0:T(8,128)(2,1)} reshape(bf16[8,28,8192]{2,1,0:T(8,128)(2,1)} %all-gather.3.cloned.1.call-done) | data formatting | bytes 7340032
  178.3 10.5 %fusion.90 = f32[224,896]{1,0:T(8,128)S(1)} fusion(bf16[224,8192]{1,0:T(8,128)(2,1)} %reshape.314, bf16[8192,896]{1,0:T(8,128)(2,1)} %param.19), kind=kOutput, calls=%fused_computation.127 | convolution fusion | flops 3288334336 | bytes 19152896 | tf_op jit(solution)/shard_map/dot_general | solution.py:151
  190.6 1.7 collective-permute-done.5
  (107 shorter events, 11.2 us)
Async XLA Ops:
  6.5 30.0 %copy-start = (s32[8,8]{1,0:T(8,128)S(1)}, s32[8,8]{1,0:T(8,128)}, u32[]{:S(2)}) copy-start(s32[8,8]{1,0:T(8,128)} %param.23) | copy-start | bytes 772
  8.2 28.6 %all-to-all-start.1 = ((bf16[8,2,3584]{2,1,0:T(2,128)(2,1)}), bf16[8,2,3584]{2,1,0:T(2,128)(2,1)S(1)}, u32[]{:S(2)}, u32[]{:S(2)}) async-start(bf16[8,2,3584]{2,1,0:T(2,128)(2,1)} %slice.138), calls=%async_computation.1 | async-start | bytes 229376 | tf_op jit(solution)/shard_map/all_to_all | solution.py:86
  15.4 6.4 %copy-start.2 = (bf16[3584,576]{0,1:T(8,128)(2,1)S(1)}, bf16[3584,576]{0,1:T(8,128)(2,1)}, u32[]{:S(2)}) copy-start(bf16[3584,576]{0,1:T(8,128)(2,1)} %param.15) | copy-start | bytes 12386308
  21.8 5.1 %copy-start.9 = (bf16[1536,3584]{1,0:T(8,128)(2,1)S(1)}, bf16[1536,3584]{1,0:T(8,128)(2,1)}, u32[]{:S(2)}) copy-start(bf16[1536,3584]{1,0:T(8,128)(2,1)} %param.12) | copy-start | bytes 33030148
  21.8 49.6 %collective-permute-start.3 = (f32[384,576]{0,1:T(8,128)}, f32[384,576]{0,1:T(8,128)}, u32[]{:S(2)}, u32[]{:S(2)}) collective-permute-start(f32[384,576]{0,1:T(8,128)} %fusion.9), channel_id=1, source_target_pairs={{0,1},{1,0},{2,3},{3,2},{4,5},{5,4},{6,7},{7,6},{8,9},{9,8},{10,11... | collective-permute-start | bytes 2654216 | tf_op jit(solution)/shard_map/ppermute | solution.py:23
  26.1 50.3 %collective-permute-start = (f32[384,576]{0,1:T(8,128)S(1)}, f32[384,576]{0,1:T(8,128)}, u32[]{:S(2)}, u32[]{:S(2)}) collective-permute-start(f32[384,576]{0,1:T(8,128)S(1)} %fusion.15), channel_id=1, source_target_pairs={{0,1},{1,0},{2,3},{3,2},{4,5},{5,4},{6,7},{7,6},{8,9},{9,8},{10,11... | collective-permute-start | bytes 2654216 | tf_op jit(solution)/shard_map/ppermute | solution.py:23
  30.1 3.8 %copy-start.6 = (bf16[14,2,12288]{2,1,0:T(2,128)(2,1)S(1)}, bf16[14,2,12288]{2,1,0:T(2,128)(2,1)}, u32[]{:S(2)}) copy-start(bf16[14,2,12288]{2,1,0:T(2,128)(2,1)} %param.14) | copy-start | bytes 2064388
  30.1 6.6 %copy-start.8 = (s32[6]{0:T(128)S(1)}, s32[6]{0:T(128)}, u32[]{:S(2)}) copy-start(s32[6]{0:T(128)} %param.21) | copy-start | bytes 76
  30.1 13.0 %slice-start.1 = ((bf16[14,2,3584]{2,1,0:T(2,128)(2,1)}), bf16[6,2,3584]{2,1,0:T(2,128)(2,1)S(1)}, s32[]{:S(2)}) async-start(bf16[14,2,3584]{2,1,0:T(2,128)(2,1)} %param.13), calls=%async_computation.4 | async-start | bytes 172032 | tf_op jit(solution)/shard_map/slice | solution.py:106
  30.1 44.4 %collective-permute-start.1 = (f32[384,576]{0,1:T(8,128)}, f32[384,576]{0,1:T(8,128)}, u32[]{:S(2)}, u32[]{:S(2)}) collective-permute-start(f32[384,576]{0,1:T(8,128)} %fusion.13), channel_id=1, source_target_pairs={{0,1},{1,0},{2,3},{3,2},{4,5},{5,4},{6,7},{7,6},{8,9},{9,8},{10,11... | collective-permute-start | bytes 2654216 | tf_op jit(solution)/shard_map/ppermute | solution.py:23
  33.4 39.6 %collective-permute-start.2 = (f32[384,576]{0,1:T(8,128)}, f32[384,576]{0,1:T(8,128)}, u32[]{:S(2)}, u32[]{:S(2)}) collective-permute-start(f32[384,576]{0,1:T(8,128)} %fusion.11), channel_id=1, source_target_pairs={{0,1},{1,0},{2,3},{3,2},{4,5},{5,4},{6,7},{7,6},{8,9},{9,8},{10,11... | collective-permute-start | bytes 2654216 | tf_op jit(solution)/shard_map/ppermute | solution.py:23
  36.8 18.0 %all-to-all-start = ((bf16[8,2,12288]{2,1,0:T(2,128)(2,1)}), bf16[8,2,12288]{2,1,0:T(2,128)(2,1)S(1)}, u32[]{:S(2)}, u32[]{:S(2)}) async-start(bf16[8,2,12288]{2,1,0:T(2,128)(2,1)} %slice.121), calls=%async_computation | async-start | bytes 786432 | tf_op jit(solution)/shard_map/all_to_all | solution.py:85
  42.9 130.6 %all-gather.3.cloned.1.call-start = ((), (), s32[]{:S(2)}) async-start(), calls=%async_computation.2 | async-start | bytes 4718592 | tf_op jit(solution)/shard_map/all_gather | solution.py:150
  43.4 5.1 %copy-start.7 = (f32[512]{0:T(512)S(1)}, f32[512]{0:T(512)}, u32[]{:S(2)}) copy-start(f32[512]{0:T(512)} %param.16) | copy-start | bytes 6148
  43.5 11.3 %slice-start = ((bf16[14,2,12288]{2,1,0:T(2,128)(2,1)}), bf16[6,2,12288]{2,1,0:T(2,128)(2,1)S(1)}, s32[]{:S(2)}) async-start(bf16[14,2,12288]{2,1,0:T(2,128)(2,1)} %param.14), calls=%async_computation.3 | async-start | bytes 589824 | tf_op jit(solution)/shard_map/slice | solution.py:121
  47.0 1.3 collective-permute-start.4
  62.3 1.8 copy-start.3
  64.0 1.6 copy-start.4
  78.3 6.5 %copy-start.5 = (bf16[8,2,64,576]{3,0,1,2:T(8,128)(2,1)S(1)}, bf16[8,2,64,576]{3,0,1,2:T(8,128)(2,1)}, u32[]{:S(2)}) copy-start(bf16[8,2,64,576]{3,0,1,2:T(8,128)(2,1)} %copy-done.4) | copy-start | bytes 3538948
  189.4 3.6 %copy-start.1 = (s32[8,8]{1,0:T(8,128)S(1)}, s32[8,8]{1,0:T(8,128)}, u32[]{:S(2)}) copy-start(s32[8,8]{1,0:T(8,128)} %param.23) | copy-start | bytes 772
  190.5 1.8 collective-permute-start.5
Sparse Core Ops, SparseCore 0:
  101.0 72.4 all-gather.2

commit v2 on v1

--- a/solution.py
+++ b/solution.py
@@ -3,6 +3,8 @@
 import jax
 import jax.numpy as jnp
 from jax import lax
+from jax.experimental import pallas as pl
+from jax.experimental.pallas import tpu as pltpu
 from jax.sharding import PartitionSpec as P
 
 ROPE = 64
@@ -58,6 +60,188 @@
     for j in range(own_keys.shape[2]):
         combined = combined + near[..., j : j + 1] * keys[:, :, j][:, :, None, None, :]
     return (combined / totals).astype(jnp.bfloat16)
+
+
+WIDE = 2
+
+
+def gather_out_kernel(
+    high,
+    h_ref,
+    w_hbm,
+    fresh_ref,
+    old_ref,
+    blocks,
+    weight,
+    total,
+    land_fresh,
+    land_old,
+    recv_sem,
+    send_sem,
+    local_sem,
+    pair_send,
+    pair_recv,
+):
+    me = lax.axis_index("pool")
+    core = lax.axis_index("tp")
+    row = lax.div(me, WIDE)
+    col = lax.rem(me, WIDE)
+    side = row * WIDE + (1 - col)
+    up, down = me + WIDE, me - WIDE
+    has_up, has_down = row < high - 1, row > 0
+    w_copy = pltpu.make_async_copy(w_hbm, weight, local_sem.at[0])
+    w_copy.start()
+
+    barrier = pltpu.get_barrier_semaphore()
+
+    def greet(target):
+        pl.semaphore_signal(
+            barrier, inc=1, device_id=target, device_id_type=pl.DeviceIdType.MESH
+        )
+
+    greet({"pool": side})
+    greet({"tp": 1 - core})
+    pl.when(has_up)(lambda: greet({"pool": up}))
+    pl.when(has_down)(lambda: greet({"pool": down}))
+    pl.semaphore_wait(barrier, 2 + has_up.astype(jnp.int32) + has_down.astype(jnp.int32))
+
+    def copy(piece, slot, way, own=False):
+        return pltpu.make_async_remote_copy(
+            src_ref=h_ref.at[piece] if own else blocks.at[piece, slot],
+            dst_ref=blocks.at[piece, slot],
+            send_sem=send_sem.at[piece, slot, way],
+            recv_sem=recv_sem.at[piece, slot],
+            device_id={"pool": (side, up, down)[way]},
+            device_id_type=pl.DeviceIdType.MESH,
+        )
+
+    for piece in range(2):
+        pl.when(has_up)(lambda: copy(piece, me, 1, True).start())
+        pl.when(has_down)(lambda: copy(piece, me, 2, True).start())
+        copy(piece, me, 0, True).start()
+        pltpu.make_async_copy(h_ref.at[piece], blocks.at[piece, me], local_sem.at[1 + piece]).start()
+
+    for step in range(1, high):
+        for piece in range(2):
+
+            @pl.when(row >= step)
+            def _():
+                slot = me - step * WIDE
+                copy(piece, slot, 0).wait_recv()
+                pl.when(has_up)(lambda: copy(piece, slot, 1).start())
+                copy(piece, slot, 0).start()
+
+            @pl.when(row + step < high)
+            def _():
+                slot = me + step * WIDE
+                copy(piece, slot, 0).wait_recv()
+                pl.when(has_down)(lambda: copy(piece, slot, 2).start())
+                copy(piece, slot, 0).start()
+
+    for piece in range(2):
+        for at in range(high):
+            copy(piece, at * WIDE + 1 - col, 0).wait_recv()
+        pltpu.make_async_copy(
+            h_ref.at[piece], blocks.at[piece, me], local_sem.at[1 + piece]
+        ).wait()
+    w_copy.wait()
+
+    total[...] = jnp.zeros_like(total)
+    depth = 1024
+    slots, rows = blocks.shape[1:3]
+
+    @pl.loop(0, weight.shape[0] // depth)
+    def _(k):
+        cut = pl.ds(pl.multiple_of(k * depth, depth), depth)
+        left = blocks[:, :, :, cut].reshape(2 * slots * rows, depth)
+        total[...] += jnp.dot(
+            left, weight[cut, :], preferred_element_type=jnp.float32
+        ).reshape(total.shape)
+
+    half_rows, half_slots = rows // 2, slots // 2
+    their_rows = pl.ds(pl.multiple_of((1 - core) * half_rows, half_rows), half_rows)
+    my_rows = pl.ds(pl.multiple_of(core * half_rows, half_rows), half_rows)
+    pair = [
+        pltpu.make_async_remote_copy(
+            src_ref=src,
+            dst_ref=dst,
+            send_sem=pair_send.at[n],
+            recv_sem=pair_recv.at[n],
+            device_id={"tp": 1 - core},
+            device_id_type=pl.DeviceIdType.MESH,
+        )
+        for n, (src, dst) in enumerate(
+            (
+                (total.at[0, :, their_rows, :], land_fresh),
+                (total.at[1, pl.ds((1 - core) * half_slots, half_slots)], land_old),
+            )
+        )
+    ]
+    for one in pair:
+        one.start()
+    pair[0].wait()
+    fresh_ref[...] = (total[0, :, my_rows, :] + land_fresh[...]).astype(fresh_ref.dtype)
+    pair[1].wait()
+    old_ref[...] = (total[1, pl.ds(core * half_slots, half_slots)] + land_old[...]).astype(
+        old_ref.dtype
+    )
+
+    for piece in range(2):
+        copy(piece, me, 0, True).wait_send()
+        pl.when(has_up)(lambda: copy(piece, me, 1, True).wait_send())
+        pl.when(has_down)(lambda: copy(piece, me, 2, True).wait_send())
+    for step in range(1, high):
+        for piece in range(2):
+
+            @pl.when(row >= step)
+            def _():
+                slot = me - step * WIDE
+                pl.when(has_up)(lambda: copy(piece, slot, 1).wait_send())
+                copy(piece, slot, 0).wait_send()
+
+            @pl.when(row + step < high)
+            def _():
+                slot = me + step * WIDE
+                pl.when(has_down)(lambda: copy(piece, slot, 2).wait_send())
+                copy(piece, slot, 0).wait_send()
+
+
+def gather_out(fresh_rows, old_rows, out_weight):
+    pool = lax.axis_size("pool")
+    rows = 2 * pool
+    n_old = old_rows.shape[0]
+    depth, cols = out_weight.shape
+    old_rows = jnp.pad(old_rows, ((0, rows - n_old), (0, 0)))
+    fresh, old = pl.pallas_call(
+        lambda *refs: gather_out_kernel(pool // WIDE, *refs),
+        out_shape=(
+            jax.ShapeDtypeStruct((pool, rows // 2, cols), jnp.float32),
+            jax.ShapeDtypeStruct((pool // 2, rows, cols), jnp.float32),
+        ),
+        in_specs=[
+            pl.BlockSpec(memory_space=pltpu.VMEM),
+            pl.BlockSpec(memory_space=pl.ANY),
+        ],
+        out_specs=[pl.BlockSpec(memory_space=pltpu.VMEM)] * 2,
+        scratch_shapes=[
+            pltpu.VMEM((2, pool, rows, depth), jnp.bfloat16),
+            pltpu.VMEM((depth, cols), jnp.bfloat16),
+            pltpu.VMEM((2, pool, rows, cols), jnp.float32),
+            pltpu.VMEM((pool, rows // 2, cols), jnp.float32),
+            pltpu.VMEM((pool // 2, rows, cols), jnp.float32),
+            pltpu.SemaphoreType.DMA((2, pool)),
+            pltpu.SemaphoreType.DMA((2, pool, 3)),
+            pltpu.SemaphoreType.DMA((3,)),
+            pltpu.SemaphoreType.DMA((2,)),
+            pltpu.SemaphoreType.DMA((2,)),
+        ],
+        compiler_params=pltpu.CompilerParams(
+            collective_id=0, has_side_effects=True, vmem_limit_bytes=40 * 2**20
+        ),
+    )(jnp.stack([fresh_rows, old_rows]), out_weight)
+    fresh = fresh.reshape(pool, pool // 2, 2, cols).transpose(1, 0, 2, 3)
+    old = old[:, :n_old].reshape(pool // 2, n_old // 2, 2, cols)
+    return jnp.concatenate([fresh, old], axis=1).reshape(-1, cols).astype(jnp.bfloat16)
 
 
 def body(
@@ -147,6 +331,8 @@
         .astype(jnp.bfloat16)
         .reshape(requests * 2, -1)
     )
+    if lax.axis_size("tp") == 2 and pool_size == 8:
+        return gather_out(head_rows[: 2 * pool_size], head_rows[2 * pool_size :], out_weight)
     gathered = lax.all_gather(head_rows, "pool", axis=0, tiled=True)
     partial_out = jnp.dot(gathered, out_weight, preferred_element_type=jnp.float32)
     cols = partial_out.shape[-1]

time: 201 us -> 152 us (0.76)
  waiting for transfers between devices: 81.5 us -> 7.41 us
  Pallas kernels: 0 us -> 55.8 us
  between operations: 14 us -> 0.66 us
  matrix products: 52.2 us -> 41.7 us
  local copies, waits for them, and re-layouts: 14.8 us -> 9.09 us
    all_gather x1 -> x0, waiting for transfers between devices: 72.6 us -> none  [body(): gathered = lax.all_gather(head_rows, 'pool', axis=0, tiled=True)]
    pallas_call x0 -> x1, Pallas kernels: none -> 55.8 us  [gather_out(): pl.pallas_call(lambda *refs: gather_out_kernel(pool // WIDE, *refs), out_...]
    dot_general x1 -> x0, matrix products: 10.5 us -> none  [body(): jnp.dot(gathered, out_weight, preferred_element_type=jnp.float32)]
    unnamed x25, local copies, waits for them, and re-layouts: 7.84 us -> 2.13 us
  transfers between devices with their start and end apart: 9 -> 7, of which waited for: 4 -> 2; matrix products, arithmetic and copies ran while one was open for 22% -> 29% of each run, Pallas kernels for 0% -> 0%
where the time goes in v2:
time: 152 us; the launch traced here: 151 us
  Pallas kernels  55.8 us (37%)
  matrix products  41.7 us (27%)
  other arithmetic  21.5 us (14%)
  starting transfers between devices  14.8 us (10%)
  local copies, waits for them, and re-layouts  9.09 us (6%)
  waiting for transfers between devices  7.41 us (5%)
    pallas_call x1, Pallas kernels, gather_out(): pl.pallas_call(lambda *refs: gather_out_kernel(pool // WIDE, *refs), out_...  55.8 us
    dot_general x4, matrix products, body(): jnp.dot(x_pre[c * rows:(c + 1) * rows], kv_weight, preferred_element_type...  17.1 us
    all_to_all x1, starting transfers between devices, body(): lax.all_to_all(x_dec[:pool_size], 'pool', split_axis=0, concat_axis=0, ti...  7.25 us
    dot_general x2, matrix products, attend(): jnp.einsum('bgihl,blc->bgihc', far.astype(jnp.bfloat16), cache[..., :lat_...  6.77 us
    broadcast_in_dim x1, other arithmetic, body(): pre_rows[None]  6.72 us
    all_to_all x1, waiting for transfers between devices, body(): lax.all_to_all(q_dec[:pool_size], 'pool', split_axis=0, concat_axis=0, ti...  6.15 us
    all_to_all x1, starting transfers between devices, body(): lax.all_to_all(q_dec[:pool_size], 'pool', split_axis=0, concat_axis=0, ti...  6.09 us
    add x5, other arithmetic, tp_sum(): return part + lax.ppermute(part, 'tp', [(0, 1), (1, 0)])  5.92 us
  transfers between devices with their start and end apart: 7, of which 2 were waited for; matrix products, arithmetic and copies ran while one was open for 29% of the time, Pallas kernels for 0%

profile of v2, /device:TPU:0, one launch (start us, length us, event | category | flops | bytes accessed | tf_op | source)
XLA Modules:
  0.0 151.0 jit_solution(17282908020449234965)
XLA Ops:
  0.0 1.6 %slice.146 = bf16[8,2,3584]{2,1,0:T(2,128)(2,1)} slice(bf16[14,2,3584]{2,1,0:T(2,128)(2,1)} %param.13), slice={[0:8], [0:2], [0:3584]} | slice | bytes 229376 | tf_op jit(solution)/shard_map/slice | solution.py:270
  1.6 7.3 %all-to-all-start.1 = ((bf16[8,2,3584]{2,1,0:T(2,128)(2,1)}), bf16[8,2,3584]{2,1,0:T(2,128)(2,1)S(1)}, u32[]{:S(2)}, u32[]{:S(2)}) async-start(bf16[8,2,3584]{2,1,0:T(2,128)(2,1)} %slice.146), calls=%async_computation.1 | async-start | bytes 229376 | tf_op jit(solution)/shard_map/all_to_all | solution.py:270
  8.9 6.4 %fusion.9 = f32[384,576]{0,1:T(8,128)} fusion(bf16[3584,576]{0,1:T(8,128)(2,1)} %param.15, bf16[1536,3584]{1,0:T(8,128)(2,1)} %param.12), kind=kOutput, calls=%fused_computation.11 | convolution fusion | flops 1585446912 | bytes 7766016 | tf_op jit(solution)/shard_map/dot_general | solution.py:278
  15.3 4.2 %fusion.15 = f32[384,576]{0,1:T(8,128)S(1)} fusion(bf16[3584,576]{0,1:T(8,128)(2,1)S(1)} %copy-done.2, bf16[1536,3584]{1,0:T(8,128)(2,1)} %param.12), kind=kOutput, calls=%fused_computation.17 | convolution fusion | flops 1585446912 | bytes 7766016 | tf_op jit(solution)/shard_map/dot_general | solution.py:278
  19.5 0.8 collective-permute-start
  20.4 3.2 %fusion.13 = f32[384,576]{0,1:T(8,128)} fusion(bf16[3584,576]{0,1:T(8,128)(2,1)S(1)} %copy-done.2, bf16[1536,3584]{1,0:T(8,128)(2,1)S(1)} %copy-done.9), kind=kOutput, calls=%fused_computation.15 | convolution fusion | flops 1585446912 | bytes 7766016 | tf_op jit(solution)/shard_map/dot_general | solution.py:278
  23.6 3.2 %fusion.11 = f32[384,576]{0,1:T(8,128)} fusion(bf16[3584,576]{0,1:T(8,128)(2,1)S(1)} %copy-done.2, bf16[1536,3584]{1,0:T(8,128)(2,1)S(1)} %copy-done.9), kind=kOutput, calls=%fused_computation.13 | convolution fusion | flops 1585446912 | bytes 7766016 | tf_op jit(solution)/shard_map/dot_general | solution.py:278
  27.4 1.0 slice.129
  29.3 0.7 bitcast_subtract_fusion
  30.3 6.1 %all-to-all-start = ((bf16[8,2,12288]{2,1,0:T(2,128)(2,1)}), bf16[8,2,12288]{2,1,0:T(2,128)(2,1)S(1)}, u32[]{:S(2)}, u32[]{:S(2)}) async-start(bf16[8,2,12288]{2,1,0:T(2,128)(2,1)} %slice.129), calls=%async_computation | async-start | bytes 786432 | tf_op jit(solution)/shard_map/all_to_all | solution.py:269
  36.7 3.5 %fusion.88 = f32[28,576]{1,0:T(8,128)S(1)} fusion(bf16[28,3584]{1,0:T(8,128)(2,1)S(1)} %reshape.311, bf16[3584,576]{0,1:T(8,128)(2,1)} %param.15), kind=kOutput, calls=%fused_computation.125 | convolution fusion | flops 115605504 | bytes 4393984 | tf_op jit(solution)/shard_map/dot_general | solution.py:291
  40.3 1.3 collective-permute-done.4
  42.1 6.1 %all-to-all-done = bf16[8,2,12288]{2,1,0:T(2,128)(2,1)S(1)} async-done(((bf16[8,2,12288]{2,1,0:T(2,128)(2,1)}), bf16[8,2,12288]{2,1,0:T(2,128)(2,1)S(1)}, u32[]{:S(2)}, u32[]{:S(2)}) %all-to-all-start) | async-done | bytes 393248 | tf_op jit(solution)/shard_map/all_to_all | solution.py:269
  48.2 0.9 pad_maximum_fusion.1
  49.1 1.0 reshape.310
  50.7 4.7 %convert_bitcast_fusion = bf16[14,2,64,512]{3,0,1,2:T(8,128)(2,1)S(1)} fusion(bf16[64,128,512]{2,1,0:T(8,128)(2,1)} %param.17, bf16[14,2,64,128]{3,2,1,0:T(8,128)(2,1)S(1)} %slice.169), kind=kOutput, calls=%fused_computation.33 | convolution fusion | flops 235798528 | bytes 10682368 | tf_op jit(solution)/shard_map/rihn,hnc->rihc/dot_general | solution.py:308
  55.9 1.6 %copy-done.3 = bf16[6,384,576]{1,2,0:T(8,128)(2,1)S(1)} copy-done((bf16[6,384,576]{1,2,0:T(8,128)(2,1)S(1)}, bf16[6,384,576]{1,2,0:T(8,128)(2,1)}, u32[]{:S(2)}) %copy-start.3) | copy-done | bytes 2654232
  57.5 0.9 fusion.85
  59.1 0.7 fusion.87
  60.7 2.6 %fusion.19 = f32[6,2,64,512]{3,2,1,0:T(8,128)S(1)} fusion(bf16[6,384,576]{1,2,0:T(8,128)(2,1)} %param.20, f32[6,2,64,384]{3,2,1,0:T(8,128)S(1)} %get-tuple-element.32, f32[6,2,64]{2,1,0:T(2,128)S(1)} %max.19), kind=kOutput, calls=%fused_computation.23 | convolution fusion | flops 302579712 | bytes 5114880 | tf_op jit(solution)/shard_map/bgihl,blc->bgihc/dot_general | solution.py:53
  63.3 1.4 fusion.27
  64.7 1.5 %add.109 = f32[384,576]{0,1:T(8,128)S(1)} add(f32[384,576]{0,1:T(8,128)} %fusion.9, f32[384,576]{0,1:T(8,128)} %collective-permute-done.3) | non-fusion elementwise | flops 221184 | bytes 2654208 | tf_op jit(solution)/shard_map/add | solution.py:25
  66.3 1.5 %add.107 = f32[384,576]{0,1:T(8,128)S(1)} add(f32[384,576]{0,1:T(8,128)} %fusion.11, f32[384,576]{0,1:T(8,128)} %collective-permute-done.2) | non-fusion elementwise | flops 221184 | bytes 2654208 | tf_op jit(solution)/shard_map/add | solution.py:25
  67.8 1.5 %add.105 = f32[384,576]{0,1:T(8,128)S(1)} add(f32[384,576]{0,1:T(8,128)} %fusion.13, f32[384,576]{0,1:T(8,128)} %collective-permute-done.1) | non-fusion elementwise | flops 221184 | bytes 2654208 | tf_op jit(solution)/shard_map/add | solution.py:25
  69.7 1.3 add.103
  71.5 6.7 %fusion.79 = bf16[1,1536,576]{1,2,0:T(8,128)(2,1)S(1)} fusion(bf16[384,64]{0,1:T(8,128)(2,1)S(1)} %slice.246, bf16[384,512]{0,1:T(8,128)(2,1)S(1)} %get-tuple-element.30, bf16[384,64]{0,1:T(8,128)(2,1)S(1)} %slice.247, bf16[384,512]{0,1:T(8,128)(2,1)S(1)} %get-tuple-element.29, bf16[384,64]{0,1:T(8,128)(2,1)S(1)} %slice.248, ...), kind=kLoop, calls=%fused_computation.117 | loop fusion | flops 14155776 | bytes 3538944 | tf_op jit(solution)/shard_map/broadcast_in_dim | solution.py:321
  78.3 2.7 %fusion.4 = (f32[8,2,64]{2,1,0:T(2,128)S(1)}, f32[8,2,64,1536]{3,2,1,0:T(8,128)S(1)}) fusion(pred[8,1536]{1,0:T(8,128)(4,1)S(1)} %fusion.68, bf16[384,64]{0,1:T(8,128)(2,1)S(1)} %slice.246, bf16[384,512]{0,1:T(8,128)(2,1)S(1)} %get-tuple-element.30, bf16[384,64]{0,1:T(8,128)(2,1)S(1)} %slice.247, bf16[384,512]{0,1:T(8,128)(2,1)S(1)} %get-tuple-element.29, ...), kind=kOutput, calls=%fused_computation.6 | convolution fusion | flops 1830812672 | bytes 9256960 | tf_op jit(solution)/shard_map/bgihc,blc->bgihl/dot_general | solution.py:40
  81.0 2.8 %fusion.6 = (bf16[8,2,64,1536]{3,2,1,0:T(8,128)(2,1)}, f32[8,2,64]{2,1,0:T(2,128)S(1)}) fusion(f32[8,2,64,1536]{3,2,1,0:T(8,128)S(1)} %get-tuple-element.36, f32[8,2,64]{2,1,0:T(2,128)S(1)} %max.18, pred[8,1536]{1,0:T(8,128)(4,1)S(1)} %fusion.68), kind=kLoop, calls=%fused_computation.8 | loop fusion | flops 7863296 | bytes 9457664 | tf_op jit(solution)/shard_map/convert_element_type | solution.py:55
  84.2 4.2 %divide_convert_fusion = bf16[8,2,64,512]{3,0,1,2:T(8,128)(2,1)S(1)} fusion(f32[8,2,64]{0,1,2:T(2,128)S(1)} %copy.69, f32[8,512]{1,0:T(8,128)S(1)} %get-tuple-element.41, f32[8,2,64]{0,1,2:T(2,128)S(1)} %copy.68, f32[8,512]{1,0:T(8,128)S(1)} %get-tuple-element.42, f32[8,2,64]{0,1,2:T(2,128)S(1)} %copy.67, bf16[1,1536,576]{1,2,0:T(8,128)(2,1)S(1)} %fusion.79, ...), kind=kOutput, calls=%fused_computation.32 | convolution fusion | flops 1613758464 | bytes 5996544 | tf_op jit(solution)/shard_map/bgihl,blc->bgihc/dot_general | solution.py:53
  88.4 4.6 %fusion.44 = bf16[14,2,64,128]{3,0,1,2:T(8,128)(2,1)S(1)} fusion(bf16[64,512,128]{2,1,0:T(8,128)(2,1)} %param.18, bf16[6,2,64,512]{3,0,1,2:T(8,128)(2,1)S(1)} %fusion.27, bf16[8,2,64,512]{3,0,1,2:T(8,128)(2,1)S(1)} %divide_convert_fusion), kind=kOutput, calls=%fused_computation.44 | convolution fusion | flops 238780416 | bytes 10682368 | tf_op jit(solution)/shard_map/rihc,hcv->rihv/dot_general | solution.py:330
  93.7 55.8 %shard_map.118 = (f32[8,8,896]{2,1,0:T(8,128)S(1)}, f32[4,16,896]{2,1,0:T(8,128)S(1)}) custom-call(bf16[2,16,8192]{2,1,0:T(8,128)(2,1)S(1)} %pad_maximum_fusion.2.refs_0_, bf16[8192,896]{1,0:T(8,128)(2,1)} %refs_1_.1), custom_call_target="tpu_custom_call" | custom-call | tf_op jit(solution)/shard_map/pallas_call | solution.py:215
  150.2 0.8 convert_element_type.55
  (109 shorter events, 7.4 us)
Async XLA Ops:
  0.0 30.0 %copy-start = (s32[8,8]{1,0:T(8,128)S(1)}, s32[8,8]{1,0:T(8,128)}, u32[]{:S(2)}) copy-start(s32[8,8]{1,0:T(8,128)} %param.23) | copy-start | bytes 772
  1.6 28.6 %all-to-all-start.1 = ((bf16[8,2,3584]{2,1,0:T(2,128)(2,1)}), bf16[8,2,3584]{2,1,0:T(2,128)(2,1)S(1)}, u32[]{:S(2)}, u32[]{:S(2)}) async-start(bf16[8,2,3584]{2,1,0:T(2,128)(2,1)} %slice.146), calls=%async_computation.1 | async-start | bytes 229376 | tf_op jit(solution)/shard_map/all_to_all | solution.py:270
  8.9 6.4 %copy-start.2 = (bf16[3584,576]{0,1:T(8,128)(2,1)S(1)}, bf16[3584,576]{0,1:T(8,128)(2,1)}, u32[]{:S(2)}) copy-start(bf16[3584,576]{0,1:T(8,128)(2,1)} %param.15) | copy-start | bytes 12386308
  15.3 5.1 %copy-start.9 = (bf16[1536,3584]{1,0:T(8,128)(2,1)S(1)}, bf16[1536,3584]{1,0:T(8,128)(2,1)}, u32[]{:S(2)}) copy-start(bf16[1536,3584]{1,0:T(8,128)(2,1)} %param.12) | copy-start | bytes 33030148
  15.3 49.4 %collective-permute-start.3 = (f32[384,576]{0,1:T(8,128)}, f32[384,576]{0,1:T(8,128)}, u32[]{:S(2)}, u32[]{:S(2)}) collective-permute-start(f32[384,576]{0,1:T(8,128)} %fusion.9), channel_id=1, source_target_pairs={{0,1},{1,0},{2,3},{3,2},{4,5},{5,4},{6,7},{7,6},{8,9},{9,8},{10,11... | collective-permute-start | bytes 2654216 | tf_op jit(solution)/shard_map/ppermute | solution.py:25
  19.5 50.1 %collective-permute-start = (f32[384,576]{0,1:T(8,128)S(1)}, f32[384,576]{0,1:T(8,128)}, u32[]{:S(2)}, u32[]{:S(2)}) collective-permute-start(f32[384,576]{0,1:T(8,128)S(1)} %fusion.15), channel_id=1, source_target_pairs={{0,1},{1,0},{2,3},{3,2},{4,5},{5,4},{6,7},{7,6},{8,9},{9,8},{10,11... | collective-permute-start | bytes 2654216 | tf_op jit(solution)/shard_map/ppermute | solution.py:25
  23.6 3.8 %copy-start.6 = (bf16[14,2,12288]{2,1,0:T(2,128)(2,1)S(1)}, bf16[14,2,12288]{2,1,0:T(2,128)(2,1)}, u32[]{:S(2)}) copy-start(bf16[14,2,12288]{2,1,0:T(2,128)(2,1)} %param.14) | copy-start | bytes 2064388
  23.6 6.6 %copy-start.8 = (s32[6]{0:T(128)S(1)}, s32[6]{0:T(128)}, u32[]{:S(2)}) copy-start(s32[6]{0:T(128)} %param.21) | copy-start | bytes 76
  23.6 12.7 %slice-start.1 = ((bf16[14,2,3584]{2,1,0:T(2,128)(2,1)}), bf16[6,2,3584]{2,1,0:T(2,128)(2,1)S(1)}, s32[]{:S(2)}) async-start(bf16[14,2,3584]{2,1,0:T(2,128)(2,1)} %param.13), calls=%async_computation.3 | async-start | bytes 172032 | tf_op jit(solution)/shard_map/slice | solution.py:290
  23.6 44.2 %collective-permute-start.1 = (f32[384,576]{0,1:T(8,128)}, f32[384,576]{0,1:T(8,128)}, u32[]{:S(2)}, u32[]{:S(2)}) collective-permute-start(f32[384,576]{0,1:T(8,128)} %fusion.13), channel_id=1, source_target_pairs={{0,1},{1,0},{2,3},{3,2},{4,5},{5,4},{6,7},{7,6},{8,9},{9,8},{10,11... | collective-permute-start | bytes 2654216 | tf_op jit(solution)/shard_map/ppermute | solution.py:25
  26.9 39.4 %collective-permute-start.2 = (f32[384,576]{0,1:T(8,128)}, f32[384,576]{0,1:T(8,128)}, u32[]{:S(2)}, u32[]{:S(2)}) collective-permute-start(f32[384,576]{0,1:T(8,128)} %fusion.11), channel_id=1, source_target_pairs={{0,1},{1,0},{2,3},{3,2},{4,5},{5,4},{6,7},{7,6},{8,9},{9,8},{10,11... | collective-permute-start | bytes 2654216 | tf_op jit(solution)/shard_map/ppermute | solution.py:25
  30.3 18.0 %all-to-all-start = ((bf16[8,2,12288]{2,1,0:T(2,128)(2,1)}), bf16[8,2,12288]{2,1,0:T(2,128)(2,1)S(1)}, u32[]{:S(2)}, u32[]{:S(2)}) async-start(bf16[8,2,12288]{2,1,0:T(2,128)(2,1)} %slice.129), calls=%async_computation | async-start | bytes 786432 | tf_op jit(solution)/shard_map/all_to_all | solution.py:269
  36.6 5.1 %copy-start.7 = (f32[512]{0:T(512)S(1)}, f32[512]{0:T(512)}, u32[]{:S(2)}) copy-start(f32[512]{0:T(512)} %param.16) | copy-start | bytes 6148
  36.7 11.5 %slice-start = ((bf16[14,2,12288]{2,1,0:T(2,128)(2,1)}), bf16[6,2,12288]{2,1,0:T(2,128)(2,1)S(1)}, s32[]{:S(2)}) async-start(bf16[14,2,12288]{2,1,0:T(2,128)(2,1)} %param.14), calls=%async_computation.2 | async-start | bytes 589824 | tf_op jit(solution)/shard_map/slice | solution.py:305
  40.2 1.3 collective-permute-start.4
  55.8 1.8 %copy-start.3 = (bf16[6,384,576]{1,2,0:T(8,128)(2,1)S(1)}, bf16[6,384,576]{1,2,0:T(8,128)(2,1)}, u32[]{:S(2)}) copy-start(bf16[6,384,576]{1,2,0:T(8,128)(2,1)} %param.20) | copy-start | bytes 7962628
  57.5 1.6 %copy-start.4 = (bf16[8,2,64,576]{3,0,1,2:T(8,128)(2,1)}, bf16[8,2,64,576]{3,0,1,2:T(8,128)(2,1)S(1)}, u32[]{:S(2)}) copy-start(bf16[8,2,64,576]{3,0,1,2:T(8,128)(2,1)S(1)} %fusion.38) | copy-start | bytes 3538948
  71.5 6.7 %copy-start.5 = (bf16[8,2,64,576]{3,0,1,2:T(8,128)(2,1)S(1)}, bf16[8,2,64,576]{3,0,1,2:T(8,128)(2,1)}, u32[]{:S(2)}) copy-start(bf16[8,2,64,576]{3,0,1,2:T(8,128)(2,1)} %copy-done.4) | copy-start | bytes 3538948
  93.7 57.2 %copy-start.1 = (s32[8,8]{1,0:T(8,128)S(1)}, s32[8,8]{1,0:T(8,128)}, u32[]{:S(2)}) copy-start(s32[8,8]{1,0:T(8,128)} %param.23) | copy-start | bytes 772

commit v3 on v2

v3 whole, which is shorter than its diff:
```python
import math

import jax
import jax.numpy as jnp
from jax import lax
from jax.experimental import pallas as pl
from jax.experimental.pallas import tpu as pltpu
from jax.sharding import PartitionSpec as P

ROPE = 64
NOPE = 128


def normalize(raw_rows, kv_gain):
    lat_width = kv_gain.shape[0]
    latent = raw_rows[..., :lat_width]
    factor = lax.rsqrt(jnp.mean(latent * latent, axis=-1, keepdims=True) + 1e-06)
    return jnp.concatenate([latent * factor * kv_gain, raw_rows[..., lat_width:]], axis=-1).astype(
        jnp.bfloat16
    )


def tp_sum(part):
    if lax.axis_size("tp") == 2:
        return part + lax.ppermute(part, "tp", [(0, 1), (1, 0)])
    return lax.psum(part, "tp")


def tp_scatter(part):
    if lax.axis_size("tp") == 2:
        half = part.shape[0] // 2
        me = lax.axis_index("tp")
        mine = lax.dynamic_slice_in_dim(part, me * half, half, 0)
        other = lax.dynamic_slice_in_dim(part, (1 - me) * half, half, 0)
        return mine + lax.ppermute(other, "tp", [(0, 1), (1, 0)])
    return lax.psum_scatter(part, "tp", scatter_dimension=0, tiled=True)


def attend_kernel(width, scaling, lo_ref, hi_ref, q_ref, own_ref, cache_ref, out_ref):
    at = pl.program_id(0)
    lo, hi = lo_ref[at], hi_ref[at]
    lat_width = out_ref.shape[-1]
    room = cache_ref.shape[-1] - width
    base = pl.multiple_of(jnp.minimum(lax.div(lo, 128) * 128, room), 128) if room else 0
    query = q_ref[0]
    own = own_ref[0]
    keys = cache_ref[0, :, pl.ds(base, width)]
    scores = jnp.dot(query, keys, preferred_element_type=jnp.float32) * scaling
    places = base + lax.broadcasted_iota(jnp.int32, scores.shape, 1)
    scores = jnp.where((places >= lo) & (places < hi), scores, -jnp.inf)
    flat = (((1,), (1,)), ((), ()))
    recent = lax.dot_general(query, own, flat, preferred_element_type=jnp.float32) * scaling
    later = lax.broadcasted_iota(jnp.int32, recent.shape, 1)
    second = lax.broadcasted_iota(jnp.int32, recent.shape, 0) >= recent.shape[0] // 2
    recent = jnp.where(later <= second.astype(jnp.int32), recent, -jnp.inf)
    highest = jnp.maximum(
        jnp.max(scores, axis=1, keepdims=True), jnp.max(recent, axis=1, keepdims=True)
    )
    far = jnp.exp(scores - highest)
    near = jnp.exp(recent - highest)
    inverse = 1.0 / (jnp.sum(far, axis=1, keepdims=True) + jnp.sum(near, axis=1, keepdims=True))
    combined = lax.dot_general(
        (far * inverse).astype(jnp.bfloat16),
        keys[:lat_width],
        flat,
        preferred_element_type=jnp.float32,
    ) + jnp.dot(
        (near * inverse).astype(jnp.bfloat16),
        own[:, :lat_width],
        preferred_element_type=jnp.float32,
    )
    out_ref[0] = combined.astype(out_ref.dtype)


def attend(cache, lo, hi, queries, own_keys, lat_width, width, scaling):
    number, steps, heads, wide = queries.shape
    shared = cache.shape[0] == 1
    own_keys = jnp.pad(own_keys, ((0, 0), (0, 16 - steps), (0, 0)))
    out = pl.pallas_call(
        lambda *refs: attend_kernel(width, scaling, *refs),
        grid_spec=pltpu.PrefetchScalarGridSpec(
            num_scalar_prefetch=2,
            grid=(number,),
            in_specs=[
                pl.BlockSpec((1, steps * heads, wide), lambda r, lo, hi: (r, 0, 0)),
                pl.BlockSpec((1, 16, wide), lambda r, lo, hi: (r, 0, 0)),
                pl.BlockSpec(
                    (1,) + cache.shape[1:], lambda r, lo, hi: (0 if shared else r, 0, 0)
                ),
            ],
            out_specs=pl.BlockSpec((1, steps * heads, lat_width), lambda r, lo, hi: (r, 0, 0)),
        ),
        out_shape=jax.ShapeDtypeStruct((number, steps * heads, lat_width), jnp.bfloat16),
        compiler_params=pltpu.CompilerParams(vmem_limit_bytes=24 * 2**20),
        cost_estimate=pl.CostEstimate(
            flops=4 * number * steps * heads * wide * width,
            bytes_accessed=2 * (cache.size + 2 * queries.size),
            transcendentals=number * steps * heads * width,
        ),
    )(lo, hi, queries.reshape(number, steps * heads, wide), own_keys, cache)
    return out.reshape(number, steps, heads, lat_width)


WIDE = 2


def gather_out_kernel(
    high,
    h_ref,
    old_hbm,
    w_hbm,
    fresh_ref,
    old_ref,
    blocks,
    old_rows,
    weight,
    total,
    land_fresh,
    land_old,
    recv_sem,
    send_sem,
    local_sem,
    pair_send,
    pair_recv,
):
    me = lax.axis_index("pool")
    core = lax.axis_index("tp")
    row = lax.div(me, WIDE)
    col = lax.rem(me, WIDE)
    side = row * WIDE + (1 - col)
    up, down = me + WIDE, me - WIDE
    has_up, has_down = row < high - 1, row > 0
    w_copy = pltpu.make_async_copy(w_hbm, weight, local_sem.at[0])
    w_copy.start()
    old_copy = pltpu.make_async_copy(old_hbm, old_rows, local_sem.at[1])
    old_copy.start()
    own_copy = pltpu.make_async_copy(h_ref, blocks.at[me], local_sem.at[2])

    barrier = pltpu.get_barrier_semaphore()

    def greet(target):
        pl.semaphore_signal(
            barrier, inc=1, device_id=target, device_id_type=pl.DeviceIdType.MESH
        )

    greet({"pool": side})
    greet({"tp": 1 - core})
    pl.when(has_up)(lambda: greet({"pool": up}))
    pl.when(has_down)(lambda: greet({"pool": down}))
    pl.semaphore_wait(barrier, 2 + has_up.astype(jnp.int32) + has_down.astype(jnp.int32))

    def copy(slot, way, own=False):
        return pltpu.make_async_remote_copy(
            src_ref=h_ref if own else blocks.at[slot],
            dst_ref=blocks.at[slot],
            send_sem=send_sem.at[slot, way],
            recv_sem=recv_sem.at[slot],
            device_id={"pool": (side, up, down)[way]},
            device_id_type=pl.DeviceIdType.MESH,
        )

    def pair_copy(n, src, dst):
        return pltpu.make_async_remote_copy(
            src_ref=src,
            dst_ref=dst,
            send_sem=pair_send.at[n],
            recv_sem=pair_recv.at[n],
            device_id={"tp": 1 - core},
            device_id_type=pl.DeviceIdType.MESH,
        )

    pl.when(has_up)(lambda: copy(me, 1, True).start())
    pl.when(has_down)(lambda: copy(me, 2, True).start())
    copy(me, 0, True).start()
    own_copy.start()
    total[...] = jnp.zeros_like(total)
    slots, rows, depth = blocks.shape
    part = depth // 8
    half_rows, half_slots = rows // 2, slots // 2
    w_copy.wait()
    old_copy.wait()

    def multiply(piece, source, first, last):
        @pl.loop(first, last)
        def _(k):
            cut = pl.ds(pl.multiple_of(k * part, part), part)
            left = source[:, :, cut].reshape(slots * rows, part)
            total[piece] += jnp.dot(
                left, weight[cut, :], preferred_element_type=jnp.float32
            ).reshape(total.shape[1:])

    bounds = [8 * n // high for n in range(high + 1)]
    for step in range(1, high):
        multiply(1, old_rows, bounds[step - 1], bounds[step])

        @pl.when(row >= step)
        def _():
            slot = me - step * WIDE
            copy(slot, 0).wait_recv()
            pl.when(has_up)(lambda: copy(slot, 1).start())
            copy(slot, 0).start()

        @pl.when(row + step < high)
        def _():
            slot = me + step * WIDE
            copy(slot, 0).wait_recv()
            pl.when(has_down)(lambda: copy(slot, 2).start())
            copy(slot, 0).start()

    multiply(1, old_rows, bounds[high - 1], 8)
    old_pair = pair_copy(1, total.at[1, pl.ds((1 - core) * half_slots, half_slots)], land_old)
    old_pair.start()
    own_copy.wait()
    for at in range(high):
        copy(at * WIDE + 1 - col, 0).wait_recv()
    multiply(0, blocks, 0, 8)
    their_rows = pl.ds(pl.multiple_of((1 - core) * half_rows, half_rows), half_rows)
    my_rows = pl.ds(pl.multiple_of(core * half_rows, half_rows), half_rows)
    fresh_pair = pair_copy(0, total.at[0, :, their_rows, :], land_fresh)
    fresh_pair.start()
    old_pair.wait()
    old_ref[...] = (total[1, pl.ds(core * half_slots, half_slots)] + land_old[...]).astype(
        old_ref.dtype
    )
    fresh_pair.wait()
    fresh_ref[...] = (total[0, :, my_rows, :] + land_fresh[...]).astype(fresh_ref.dtype)

    copy(me, 0, True).wait_send()
    pl.when(has_up)(lambda: copy(me, 1, True).wait_send())
    pl.when(has_down)(lambda: copy(me, 2, True).wait_send())
    for step in range(1, high):

        @pl.when(row >= step)
        def _():
            slot = me - step * WIDE
            pl.when(has_up)(lambda: copy(slot, 1).wait_send())
            copy(slot, 0).wait_send()

        @pl.when(row + step < high)
        def _():
            slot = me + step * WIDE
            pl.when(has_down)(lambda: copy(slot, 2).wait_send())
            copy(slot, 0).wait_send()


def gather_out(fresh_rows, old_rows, n_old, out_weight):
    pool = lax.axis_size("pool")
    rows = 2 * pool
    depth, cols = out_weight.shape
    fresh, old = pl.pallas_call(
        lambda *refs: gather_out_kernel(pool // WIDE, *refs),
        out_shape=(
            jax.ShapeDtypeStruct((pool, rows // 2, cols), jnp.float32),
            jax.ShapeDtypeStruct((pool // 2, rows, cols), jnp.float32),
        ),
        in_specs=[
            pl.BlockSpec(memory_space=pltpu.VMEM),
            pl.BlockSpec(memory_space=pl.ANY),
            pl.BlockSpec(memory_space=pl.ANY),
        ],
        out_specs=[pl.BlockSpec(memory_space=pltpu.VMEM)] * 2,
        scratch_shapes=[
            pltpu.VMEM((pool, rows, depth), jnp.bfloat16),
            pltpu.VMEM((pool, rows, depth), jnp.bfloat16),
            pltpu.VMEM((depth, cols), jnp.bfloat16),
            pltpu.VMEM((2, pool, rows, cols), jnp.float32),
            pltpu.VMEM((pool, rows // 2, cols), jnp.float32),
            pltpu.VMEM((pool // 2, rows, cols), jnp.float32),
            pltpu.SemaphoreType.DMA((pool,)),
            pltpu.SemaphoreType.DMA((pool, 3)),
            pltpu.SemaphoreType.DMA((3,)),
            pltpu.SemaphoreType.DMA((2,)),
            pltpu.SemaphoreType.DMA((2,)),
        ],
        compiler_params=pltpu.CompilerParams(
            collective_id=0, has_side_effects=True, vmem_limit_bytes=40 * 2**20
        ),
    )(fresh_rows, old_rows, out_weight)
    fresh = fresh.reshape(pool, pool // 2, 2, cols).transpose(1, 0, 2, 3)
    old = old[:, :n_old].reshape(pool // 2, n_old // 2, 2, cols)
    return jnp.concatenate([fresh, old], axis=1).reshape(-1, cols).astype(jnp.bfloat16)


def body(
    x_pre,
    x_dec,
    q_dec,
    kv_weight,
    kv_gain,
    up_key,
    up_value,
    out_weight,
    old_cache,
    old_lens,
    prompt_lens,
    owners,
):
    pool_size = lax.axis_size("pool")
    own_pool = lax.axis_index("pool")
    requests = x_dec.shape[0]
    model_part = x_pre.shape[1]
    heads_here = up_key.shape[0]
    lat_width = kv_gain.shape[0]
    scaling = 1.0 / math.sqrt(NOPE + ROPE)

    query_cols = q_dec.shape[-1]
    sent = jnp.concatenate([q_dec[:pool_size], x_dec[:pool_size]], axis=-1)
    arrived = lax.all_to_all(sent, "pool", split_axis=0, concat_axis=0, tiled=True)
    fresh_q, fresh_x = arrived[..., :query_cols], arrived[..., query_cols:]

    x_rows = jnp.concatenate([fresh_x, x_dec[pool_size:]], axis=0).reshape(-1, model_part)
    dec_raw = tp_sum(jnp.dot(x_rows, kv_weight, preferred_element_type=jnp.float32))
    dec_keys = normalize(dec_raw, kv_gain).reshape(requests, 2, -1)
    q_rows = jnp.concatenate([fresh_q, q_dec[pool_size:]], axis=0).reshape(
        requests, 2, heads_here, NOPE + ROPE
    )
    absorbed = jnp.einsum(
        "rihn,hnc->rihc", q_rows[..., :NOPE], up_key, preferred_element_type=jnp.float32
    )
    full_query = jnp.concatenate([absorbed.astype(jnp.bfloat16), q_rows[..., NOPE:]], axis=-1)

    def lift(combined):
        return (
            jnp.einsum("rihc,hcv->rihv", combined, up_value, preferred_element_type=jnp.float32)
            .astype(jnp.bfloat16)
            .reshape(combined.shape[0] * 2, -1)
        )

    old_rows = lift(
        attend(
            old_cache.transpose(0, 2, 1),
            jnp.zeros_like(old_lens),
            old_lens,
            full_query[pool_size:],
            dec_keys[pool_size:],
            lat_width,
            old_cache.shape[1],
            scaling,
        )
    )
    n_old = old_rows.shape[0]
    old_rows = jnp.pad(old_rows, ((0, 2 * pool_size - n_old), (0, 0)))
    all_old = lax.all_gather(old_rows, "pool", axis=0, tiled=False)

    chunks = 4
    rows = x_pre.shape[0] // chunks
    late_weight, _ = lax.optimization_barrier((kv_weight, old_rows))
    pre_rows = jnp.concatenate(
        [
            normalize(
                tp_sum(
                    jnp.dot(
                        x_pre[c * rows : (c + 1) * rows],
                        late_weight if c else kv_weight,
                        preferred_element_type=jnp.float32,
                    )
                ),
                kv_gain,
            )
            for c in range(chunks)
        ],
        axis=0,
    )

    my_lengths = lax.dynamic_index_in_dim(prompt_lens, own_pool, 0, keepdims=False)
    my_owners = lax.dynamic_index_in_dim(owners, own_pool, 0, keepdims=False)
    targets = jnp.arange(pool_size, dtype=jnp.int32)
    chosen = my_owners[:, None] == targets[None, :]
    begins = jnp.cumsum(my_lengths) - my_lengths
    start = jnp.sum(jnp.where(chosen, begins[:, None], 0), axis=0)
    count = jnp.sum(jnp.where(chosen, my_lengths[:, None], 0), axis=0)
    longest = 2 * x_pre.shape[0] // pool_size
    window = min(-(-longest // 128) * 128 + 128, x_pre.shape[0])
    fresh_rows = lift(
        attend(
            pre_rows.T[None],
            start,
            start + count,
            full_query[:pool_size],
            dec_keys[:pool_size],
            lat_width,
            window,
            scaling,
        )
    )
    if lax.axis_size("tp") == 2 and pool_size == 8:
        return gather_out(fresh_rows, all_old, n_old, out_weight)
    all_fresh = lax.all_gather(fresh_rows, "pool", axis=0, tiled=False)
    partial_out = jnp.dot(
        jnp.concatenate([all_fresh, all_old], axis=1), out_weight, preferred_element_type=jnp.float32
    )
    cols = partial_out.shape[-1]
    partial_out = partial_out.reshape(pool_size, 2 * pool_size, 2, cols)
    partial_out = jnp.concatenate(
        [
            partial_out[:, :pool_size].transpose(1, 0, 2, 3),
            partial_out[:, pool_size : pool_size + n_old // 2],
        ],
        axis=1,
    ).reshape(-1, cols)
    return tp_scatter(partial_out).astype(jnp.bfloat16)


def solution(mesh):
    placed = (
        P(("groups", "pool"), "tp"),
        P(("groups", "pool"), None, "tp"),
        P(("groups", "pool"), None, "tp"),
        P("tp", None),
        P(),
        P("tp", None, None),
        P("tp", None, None),
        P("tp", "pool"),
        P(("groups", "pool"), None, None),
        P(("groups", "pool")),
        P("groups", None),
        P("groups", None),
    )
    return jax.shard_map(
        body, mesh=mesh, in_specs=placed, out_specs=P(("groups", "tp"), "pool"), check_vma=False
    )
```

time: 152 us -> 159 us (1.046)
  waiting for transfers between devices: 7.41 us -> 24 us
  between operations: 0.66 us -> 13.9 us
  Pallas kernels: 55.8 us -> 43.6 us
  starting transfers between devices: 14.8 us -> 8.37 us
  other arithmetic: 21.5 us -> 17.8 us
  matrix products: 41.7 us -> 38.9 us
  local copies, waits for them, and re-layouts: 9.09 us -> 11.7 us
    pallas_call x1, Pallas kernels: 55.8 us -> 30.8 us  [gather_out(): pl.pallas_call(lambda *refs: gather_out_kernel(pool // WIDE, *refs), out_...]
    all_gather x0 -> x1, waiting for transfers between devices: none -> 17.1 us  [body(): all_old = lax.all_gather(old_rows, 'pool', axis=0, tiled=False)]
    pallas_call x0 -> x2, Pallas kernels: none -> 12.9 us  [attend(): pl.pallas_call(lambda *refs: attend_kernel(width, scaling, *refs), grid_s...]
    all_to_all x2 -> x1, starting transfers between devices: 13.3 us -> 7.25 us  [body(): lax.all_to_all(sent, 'pool', split_axis=0, concat_axis=0, tiled=True)]
    convert_element_type x4 -> x0, other arithmetic: 4.21 us -> none  [the longest x1 2.79 us: attend(): far.astype(jnp.bfloat16)]
    dot_general x11 -> x6, matrix products: 33.5 us -> 30.8 us  [the longest x4 24 us: body(): jnp.dot(x_pre[c * rows:(c + 1) * rows], late_weight if c else kv_weight,...]
    unnamed x25 -> x26, local copies, waits for them, and re-layouts: 2.13 us -> 4.58 us
    all_to_all x2 -> x1, waiting for transfers between devices: 6.15 us -> 6.9 us  [body(): lax.all_to_all(sent, 'pool', split_axis=0, concat_axis=0, tiled=True)]
  transfers between devices with their start and end apart: 7 -> 7, of which waited for: 2 -> 2; matrix products, arithmetic and copies ran while one was open for 29% -> 38% of each run, Pallas kernels for 0% -> 8%
where the time goes in v3:
time: 159 us; the launch traced here: 158 us
  Pallas kernels  43.6 us (27%)
  matrix products  38.9 us (24%)
  waiting for transfers between devices  24 us (15%)
  other arithmetic  17.8 us (11%)
  between operations  13.9 us (9%)
  local copies, waits for them, and re-layouts  11.7 us (7%)
  starting transfers between devices  8.37 us (5%)
    pallas_call x1, Pallas kernels, gather_out(): pl.pallas_call(lambda *refs: gather_out_kernel(pool // WIDE, *refs), out_...  30.8 us
    dot_general x4, matrix products, body(): jnp.dot(x_pre[c * rows:(c + 1) * rows], late_weight if c else kv_weight,...  24 us
    all_gather x1, waiting for transfers between devices, body(): all_old = lax.all_gather(old_rows, 'pool', axis=0, tiled=False)  17.1 us
    pallas_call x2, Pallas kernels, attend(): pl.pallas_call(lambda *refs: attend_kernel(width, scaling, *refs), grid_s...  12.9 us
    all_to_all x1, starting transfers between devices, body(): lax.all_to_all(sent, 'pool', split_axis=0, concat_axis=0, tiled=True)  7.25 us
    all_to_all x1, waiting for transfers between devices, body(): lax.all_to_all(sent, 'pool', split_axis=0, concat_axis=0, tiled=True)  6.9 us
    dot_general x2, matrix products, lift(): jnp.einsum('rihc,hcv->rihv', combined, up_value, preferred_element_type=j...  6.78 us
    broadcast_in_dim x1, other arithmetic, body(): pre_rows.T[None]  6.5 us
  transfers between devices with their start and end apart: 7, of which 2 were waited for; matrix products, arithmetic and copies ran while one was open for 38% of the time, Pallas kernels for 8%

profile of v3, /device:TPU:0, one launch (start us, length us, event | category | flops | bytes accessed | tf_op | source)
XLA Modules:
  0.0 158.4 jit_solution(16351256375180997798)
XLA Ops:
  6.5 1.0 slice.94
  7.5 1.3 slice.93
  8.8 1.2 pad_maximum_fusion.2
  10.0 7.3 %all-to-all-start = ((bf16[8,2,15872]{2,1,0:T(2,128)(2,1)}), bf16[8,2,15872]{2,1,0:T(2,128)(2,1)S(1)}, u32[]{:S(2)}, u32[]{:S(2)}) async-start(bf16[8,2,15872]{2,1,0:T(2,128)(2,1)} %pad_maximum_fusion.2), calls=%async_computation | async-start | bytes 1015808 | tf_op jit(solution)/shard_map/all_to_all | solution.py:308
  17.4 6.3 %fusion.12 = f32[384,576]{0,1:T(8,128)} fusion(bf16[3584,576]{0,1:T(8,128)(2,1)} %param.15, bf16[1536,3584]{1,0:T(8,128)(2,1)} %param.12), kind=kOutput, calls=%fused_computation.12 | convolution fusion | flops 1585446912 | bytes 7766016 | tf_op jit(solution)/shard_map/dot_general | solution.py:352
  23.6 0.7 fusion.43
  24.5 6.9 %all-to-all-done = bf16[8,2,15872]{2,1,0:T(2,128)(2,1)S(1)} async-done(((bf16[8,2,15872]{2,1,0:T(2,128)(2,1)}), bf16[8,2,15872]{2,1,0:T(2,128)(2,1)S(1)}, u32[]{:S(2)}, u32[]{:S(2)}) %all-to-all-start) | async-done | bytes 507936 | tf_op jit(solution)/shard_map/all_to_all | solution.py:308
  31.7 0.5 copy-done.7
  32.2 0.9 pad_maximum_fusion.1
  33.1 1.0 reshape.116
  35.1 3.4 %fusion.45 = f32[28,576]{1,0:T(8,128)S(1)} fusion(bf16[28,3584]{1,0:T(8,128)(2,1)S(1)} %reshape.118, bf16[3584,576]{0,1:T(8,128)(2,1)} %param.15), kind=kOutput, calls=%fused_computation.68 | convolution fusion | flops 115605504 | bytes 4393984 | tf_op jit(solution)/shard_map/dot_general | solution.py:312
  38.6 4.7 %convert_bitcast_fusion = bf16[14,2,64,512]{3,0,1,2:T(8,128)(2,1)S(1)} fusion(bf16[64,128,512]{2,1,0:T(8,128)(2,1)} %param.17, bf16[14,2,64,128]{3,2,1,0:T(8,128)(2,1)S(1)} %slice.123), kind=kOutput, calls=%fused_computation.16 | convolution fusion | flops 235798528 | bytes 10682368 | tf_op jit(solution)/shard_map/rihn,hnc->rihc/dot_general | solution.py:317
  44.3 1.7 %copy-done.1 = bf16[6,384,576]{1,2,0:T(8,128)(2,1)S(1)} copy-done((bf16[6,384,576]{1,2,0:T(8,128)(2,1)S(1)}, bf16[6,384,576]{1,2,0:T(8,128)(2,1)}, u32[]{:S(2)}) %copy-start.1) | copy-done | bytes 2654232
  46.0 5.3 %shard_map.118 = bf16[6,128,512]{2,1,0:T(8,128)(2,1)S(1)} custom-call(s32[6]{0:T(128)S(1)} %broadcast_7_refs_0_.2.refs_0_, s32[6]{0:T(128)S(1)} %copy-done.3, bf16[6,128,576]{2,1,0:T(8,128)(2,1)S(1)} %bitcast.71, bf16[6,16,576]{2,1,0:T(8,128)(2,1)S(1)} %pad.13.refs_3_, bf16[6,576,384]{2,1,0:T(8,128)(2,1)S(1)} %bitcast.73), custom_call_target="tpu_custom_call" | custom-call | flops 679477248 | bytes 4423680 | tf_op jit(solution)/shard_map/pallas_call | solution.py:79
  51.4 5.2 %fusion.35 = bf16[6,2,64,128]{3,0,1,2:T(8,128)(2,1)S(1)} fusion(bf16[64,512,128]{2,1,0:T(8,128)(2,1)} %param.18, bf16[6,2,64,512]{3,2,1,0:T(8,128)(2,1)S(1)} %bitcast.70), kind=kOutput, calls=%fused_computation.26 | convolution fusion | flops 100761600 | bytes 9371648 | tf_op jit(solution)/shard_map/rihc,hcv->rihv/dot_general | solution.py:324
  56.9 0.7 pad.14
  57.6 6.4 %fusion.22 = f32[384,576]{0,1:T(8,128)} fusion(bf16[3584,576]{0,1:T(8,128)(2,1)} %param.15, bf16[1536,3584]{1,0:T(8,128)(2,1)} %param.12), kind=kOutput, calls=%fused_computation.20 | convolution fusion | flops 1585446912 | bytes 7766016 | tf_op jit(solution)/shard_map/dot_general | solution.py:352
  64.1 5.0 %fusion.16 = f32[384,576]{0,1:T(8,128)} fusion(bf16[3584,576]{0,1:T(8,128)(2,1)S(1)} %copy-done.6, bf16[1536,3584]{1,0:T(8,128)(2,1)} %param.12), kind=kOutput, calls=%fused_computation.18 | convolution fusion | flops 1585446912 | bytes 7766016 | tf_op jit(solution)/shard_map/dot_general | solution.py:352
  69.1 6.3 %fusion.19 = f32[384,576]{0,1:T(8,128)} fusion(bf16[3584,576]{0,1:T(8,128)(2,1)} %param.15, bf16[1536,3584]{1,0:T(8,128)(2,1)} %param.12), kind=kOutput, calls=%fused_computation.19 | convolution fusion | flops 1585446912 | bytes 7766016 | tf_op jit(solution)/shard_map/dot_general | solution.py:352
  75.4 0.5 collective-permute-start.4
  76.4 0.7 bitcast_subtract_fusion
  77.2 1.5 add.73
  79.4 1.5 add.79
  81.0 1.5 add.77
  82.5 1.5 add.75
  84.8 6.5 %maximum_bitcast_fusion.refs_4_ = bf16[1,576,1536]{2,1,0:T(8,128)(2,1)S(1)} fusion(bf16[384,64]{0,1:T(8,128)(2,1)S(1)} %slice.184, bf16[384,512]{0,1:T(8,128)(2,1)S(1)} %get-tuple-element.18, bf16[384,64]{0,1:T(8,128)(2,1)S(1)} %slice.185, bf16[384,512]{0,1:T(8,128)(2,1)S(1)} %get-tuple-element.17, bf16[384,64]{0,1:T(8,128)(2,1)S(1)} %slice.186, ...), kind=kLoop, calls=%fused_computation.17 | loop fusion | flops 14155776 | bytes 3538944 | tf_op jit(solution)/shard_map/broadcast_in_dim | solution.py:376
  91.3 7.5 %shard_map.119 = bf16[8,128,512]{2,1,0:T(8,128)(2,1)S(1)} custom-call(s32[8]{0:T(128)S(1)} %get-tuple-element.12.refs_0_, s32[8]{0:T(128)S(1)} %add.70.refs_1_, bf16[8,128,576]{2,1,0:T(8,128)(2,1)S(1)} %bitcast.75, bf16[8,16,576]{2,1,0:T(8,128)(2,1)S(1)} %pad.12.refs_3_, bf16[1,576,1536]{2,1,0:T(8,128)(2,1)S(1)} %maximum_bitcast_fusion.refs_4_), custom_call_target="tpu_custom_call" | custom-call | flops 1207959552 | bytes 4128768 | tf_op jit(solution)/shard_map/pallas_call | solution.py:79
  98.9 1.5 fusion.32
  100.7 17.1 %all-gather.3.cloned.1.call-done = bf16[128,8192]{1,0:T(8,128)(2,1)} async-done(((bf16[16,8192]{1,0:T(8,128)(2,1)}), bf16[128,8192]{1,0:T(8,128)(2,1)}) %all-gather.3.cloned.1.call-update) | async-done | bytes 2097168 | tf_op jit(solution)/shard_map/all_gather | solution.py:343
  117.8 1.6 %copy-done.2 = bf16[128,8192]{1,0:T(8,128)(2,1)S(1)} copy-done((bf16[128,8192]{1,0:T(8,128)(2,1)S(1)}, bf16[128,8192]{1,0:T(8,128)(2,1)}, u32[]{:S(2)}) %copy-start.2) | copy-done | bytes 2097176
  119.4 30.8 %shard_map.120 = (f32[8,8,896]{2,1,0:T(8,128)S(1)}, f32[4,16,896]{2,1,0:T(8,128)S(1)}) custom-call(bf16[16,8192]{1,0:T(8,128)(2,1)S(1)} %bitcast.76, bf16[8,16,8192]{2,1,0:T(8,128)(2,1)S(1)} %bitcast.74, bf16[8192,896]{1,0:T(8,128)(2,1)} %refs_2_.1), custom_call_target="tpu_custom_call" | custom-call | tf_op jit(solution)/shard_map/pallas_call | solution.py:250
  150.8 0.8 convert_element_type.39
  (88 shorter events, 5.3 us)
Async XLA Ops:
  6.5 70.5 %copy-start = (s32[8,8]{1,0:T(8,128)S(1)}, s32[8,8]{1,0:T(8,128)}, u32[]{:S(2)}) copy-start(s32[8,8]{1,0:T(8,128)} %param.23) | copy-start | bytes 772
  10.0 21.4 %all-to-all-start = ((bf16[8,2,15872]{2,1,0:T(2,128)(2,1)}), bf16[8,2,15872]{2,1,0:T(2,128)(2,1)S(1)}, u32[]{:S(2)}, u32[]{:S(2)}) async-start(bf16[8,2,15872]{2,1,0:T(2,128)(2,1)} %pad_maximum_fusion.2), calls=%async_computation | async-start | bytes 1015808 | tf_op jit(solution)/shard_map/all_to_all | solution.py:308
  17.3 14.9 %slice-start.3 = ((bf16[14,2,12288]{2,1,0:T(2,128)(2,1)}), bf16[6,2,12288]{2,1,0:T(2,128)(2,1)S(1)}, s32[]{:S(2)}) async-start(bf16[14,2,12288]{2,1,0:T(2,128)(2,1)} %param.14), calls=%async_computation.5 | async-start | bytes 589824 | tf_op jit(solution)/shard_map/slice | solution.py:314
  17.3 100.5 %all-gather.3.cloned.1.call-start = ((), (), s32[]{:S(2)}) async-start(), calls=%async_computation.1 | async-start | bytes 2359296 | tf_op jit(solution)/shard_map/all_gather | solution.py:343
  23.6 53.6 %collective-permute-start.1 = (f32[384,576]{0,1:T(8,128)}, f32[384,576]{0,1:T(8,128)}, u32[]{:S(2)}, u32[]{:S(2)}) collective-permute-start(f32[384,576]{0,1:T(8,128)} %fusion.12), channel_id=1, source_target_pairs={{0,1},{1,0},{2,3},{3,2},{4,5},{5,4},{6,7},{7,6},{8,9},{9,8},{10,11... | collective-permute-start | bytes 2654216 | tf_op jit(solution)/shard_map/ppermute | solution.py:25
  23.6 11.1 %slice-start.4 = ((bf16[14,2,3584]{2,1,0:T(2,128)(2,1)}), bf16[6,2,3584]{2,1,0:T(2,128)(2,1)S(1)}, s32[]{:S(2)}) async-start(bf16[14,2,3584]{2,1,0:T(2,128)(2,1)} %param.13), calls=%async_computation.6 | async-start | bytes 172032 | tf_op jit(solution)/shard_map/slice | solution.py:311
  31.4 0.8 copy-start.7
  33.1 1.6 slice-start.2
  34.7 8.7 %copy-start.4 = (bf16[14,2,64,64]{3,0,1,2:T(8,128)(2,1)}, bf16[14,2,64,64]{3,0,1,2:T(8,128)(2,1)S(1)}, u32[]{:S(2)}) copy-start(bf16[14,2,64,64]{3,0,1,2:T(8,128)(2,1)S(1)} %copy.45) | copy-start | bytes 688132
  38.5 5.4 %collective-permute-start = (f32[28,576]{1,0:T(8,128)S(1)}, f32[28,576]{1,0:T(8,128)S(1)}, u32[]{:S(2)}, u32[]{:S(2)}) collective-permute-start(f32[28,576]{1,0:T(8,128)S(1)} %fusion.45), channel_id=1, source_target_pairs={{0,1},{1,0},{2,3},{3,2},{4,5},{5,4},{6,7},{7,6},{8,9},{9,8},{10,11... | collective-permute-start | bytes 193544 | tf_op jit(solution)/shard_map/ppermute | solution.py:25
  43.4 0.8 copy-start.8
  43.4 0.9 copy-start.3
  44.3 1.8 %copy-start.1 = (bf16[6,384,576]{1,2,0:T(8,128)(2,1)S(1)}, bf16[6,384,576]{1,2,0:T(8,128)(2,1)}, u32[]{:S(2)}) copy-start(bf16[6,384,576]{1,2,0:T(8,128)(2,1)} %param.20) | copy-start | bytes 7962628
  57.6 6.4 %copy-start.6 = (bf16[3584,576]{0,1:T(8,128)(2,1)S(1)}, bf16[3584,576]{0,1:T(8,128)(2,1)}, u32[]{:S(2)}) copy-start(bf16[3584,576]{0,1:T(8,128)(2,1)} %param.15) | copy-start | bytes 12386308
  75.4 3.5 %copy-start.5 = (bf16[14,2,64,64]{3,0,1,2:T(8,128)(2,1)S(1)}, bf16[14,2,64,64]{3,0,1,2:T(8,128)(2,1)}, u32[]{:S(2)}) copy-start(bf16[14,2,64,64]{3,0,1,2:T(8,128)(2,1)} %copy-done.4) | copy-start | bytes 688132
  75.4 4.0 %collective-permute-start.4 = (f32[384,576]{0,1:T(8,128)}, f32[384,576]{0,1:T(8,128)}, u32[]{:S(2)}, u32[]{:S(2)}) collective-permute-start(f32[384,576]{0,1:T(8,128)} %fusion.22), channel_id=1, source_target_pairs={{0,1},{1,0},{2,3},{3,2},{4,5},{5,4},{6,7},{7,6},{8,9},{9,8},{10,11... | collective-permute-start | bytes 2654216 | tf_op jit(solution)/shard_map/ppermute | solution.py:25
  75.9 6.6 %collective-permute-start.2 = (f32[384,576]{0,1:T(8,128)}, f32[384,576]{0,1:T(8,128)}, u32[]{:S(2)}, u32[]{:S(2)}) collective-permute-start(f32[384,576]{0,1:T(8,128)} %fusion.16), channel_id=1, source_target_pairs={{0,1},{1,0},{2,3},{3,2},{4,5},{5,4},{6,7},{7,6},{8,9},{9,8},{10,11... | collective-permute-start | bytes 2654216 | tf_op jit(solution)/shard_map/ppermute | solution.py:25
  75.9 5.1 %collective-permute-start.3 = (f32[384,576]{0,1:T(8,128)}, f32[384,576]{0,1:T(8,128)}, u32[]{:S(2)}, u32[]{:S(2)}) collective-permute-start(f32[384,576]{0,1:T(8,128)} %fusion.19), channel_id=1, source_target_pairs={{0,1},{1,0},{2,3},{3,2},{4,5},{5,4},{6,7},{7,6},{8,9},{9,8},{10,11... | collective-permute-start | bytes 2654216 | tf_op jit(solution)/shard_map/ppermute | solution.py:25
  84.1 14.8 %slice-start = ((s8[8388608]{0:T(1024)(128)(4,1)}), s8[4194304]{0:T(1024)(128)(4,1)S(1)}, s32[]{:S(2)}) async-start(s8[8388608]{0:T(1024)(128)(4,1)} %bitcast.77), calls=%async_computation.2 | async-start | bytes 8388608
  84.8 14.1 %slice-start.1 = ((s8[8388608]{0:T(1024)(128)(4,1)}), s8[4194304]{0:T(1024)(128)(4,1)S(1)}, s32[]{:S(2)}) async-start(s8[8388608]{0:T(1024)(128)(4,1)} %bitcast.77), calls=%async_computation.3 | async-start | bytes 8388608
  117.8 1.6 %copy-start.2 = (bf16[128,8192]{1,0:T(8,128)(2,1)S(1)}, bf16[128,8192]{1,0:T(8,128)(2,1)}, u32[]{:S(2)}) copy-start(bf16[128,8192]{1,0:T(8,128)(2,1)} %all-gather.3.cloned.1.call-done) | copy-start | bytes 6291460
Sparse Core Ops, SparseCore 0:
  69.2 48.5 all-gather.2

commit v4 on v3

--- a/solution.py
+++ b/solution.py
@@ -13,11 +13,12 @@
 
 def normalize(raw_rows, kv_gain):
     lat_width = kv_gain.shape[0]
+    rest = raw_rows.shape[-1] - lat_width
     latent = raw_rows[..., :lat_width]
     factor = lax.rsqrt(jnp.mean(latent * latent, axis=-1, keepdims=True) + 1e-06)
-    return jnp.concatenate([latent * factor * kv_gain, raw_rows[..., lat_width:]], axis=-1).astype(
-        jnp.bfloat16
-    )
+    inside = jnp.arange(raw_rows.shape[-1]) < lat_width
+    gain = jnp.concatenate([kv_gain, jnp.ones((rest,), kv_gain.dtype)])
+    return (raw_rows * jnp.where(inside, factor, 1.0) * gain).astype(jnp.bfloat16)
 
 
 def tp_sum(part):
@@ -102,6 +103,24 @@
 
 
 WIDE = 2
+
+
+def flip(index, bits):
+    for bit in (1, 2, 4):
+        if bits & bit:
+            index = index + bit - 2 * bit * lax.rem(lax.div(index, bit), 2)
+    return index
+
+
+def exchange_old(rows):
+    everyone = range(lax.axis_size("pool"))
+    swap = lambda block, n: lax.ppermute(block, "pool", [(i, i ^ n) for i in everyone])
+    across = {0: rows}
+    for n in (2, 4, 6):
+        across[n] = swap(rows, n)
+    for n in (0, 2, 4, 6):
+        across[n + 1] = swap(across[n], 1)
+    return [across[n] for n in everyone]
 
 
 def gather_out_kernel(
@@ -132,9 +151,12 @@
     has_up, has_down = row < high - 1, row > 0
     w_copy = pltpu.make_async_copy(w_hbm, weight, local_sem.at[0])
     w_copy.start()
-    old_copy = pltpu.make_async_copy(old_hbm, old_rows, local_sem.at[1])
-    old_copy.start()
-    own_copy = pltpu.make_async_copy(h_ref, blocks.at[me], local_sem.at[2])
+    own_copy = pltpu.make_async_copy(h_ref, blocks.at[me], local_sem.at[1])
+    old_copies = []
+    for n, ref in enumerate(old_hbm):
+        owner = flip(me, n)
+        old_copies.append(pltpu.make_async_copy(ref, old_rows.at[owner], local_sem.at[2 + n]))
+        old_copies[-1].start()
 
     barrier = pltpu.get_barrier_semaphore()
 
@@ -178,7 +200,8 @@
     part = depth // 8
     half_rows, half_slots = rows // 2, slots // 2
     w_copy.wait()
-    old_copy.wait()
+    for one in old_copies:
+        one.wait()
 
     def multiply(piece, source, first, last):
         @pl.loop(first, last)
@@ -248,15 +271,16 @@
     rows = 2 * pool
     depth, cols = out_weight.shape
     fresh, old = pl.pallas_call(
-        lambda *refs: gather_out_kernel(pool // WIDE, *refs),
+        lambda h, *refs: gather_out_kernel(
+            pool // WIDE, h, refs[:pool], refs[pool], *refs[pool + 1 :]
+        ),
         out_shape=(
             jax.ShapeDtypeStruct((pool, rows // 2, cols), jnp.float32),
             jax.ShapeDtypeStruct((pool // 2, rows, cols), jnp.float32),
         ),
         in_specs=[
             pl.BlockSpec(memory_space=pltpu.VMEM),
-            pl.BlockSpec(memory_space=pl.ANY),
-            pl.BlockSpec(memory_space=pl.ANY),
+            *[pl.BlockSpec(memory_space=pl.ANY)] * (pool + 1),
         ],
         out_specs=[pl.BlockSpec(memory_space=pltpu.VMEM)] * 2,
         scratch_shapes=[
@@ -268,14 +292,14 @@
             pltpu.VMEM((pool // 2, rows, cols), jnp.float32),
             pltpu.SemaphoreType.DMA((pool,)),
             pltpu.SemaphoreType.DMA((pool, 3)),
-            pltpu.SemaphoreType.DMA((3,)),
+            pltpu.SemaphoreType.DMA((2 + pool,)),
             pltpu.SemaphoreType.DMA((2,)),
             pltpu.SemaphoreType.DMA((2,)),
         ],
         compiler_params=pltpu.CompilerParams(
             collective_id=0, has_side_effects=True, vmem_limit_bytes=40 * 2**20
         ),
-    )(fresh_rows, old_rows, out_weight)
+    )(fresh_rows, *old_rows, out_weight)
     fresh = fresh.reshape(pool, pool // 2, 2, cols).transpose(1, 0, 2, 3)
     old = old[:, :n_old].reshape(pool // 2, n_old // 2, 2, cols)
     return jnp.concatenate([fresh, old], axis=1).reshape(-1, cols).astype(jnp.bfloat16)
@@ -340,7 +364,11 @@
     )
     n_old = old_rows.shape[0]
     old_rows = jnp.pad(old_rows, ((0, 2 * pool_size - n_old), (0, 0)))
-    all_old = lax.all_gather(old_rows, "pool", axis=0, tiled=False)
+    small = lax.axis_size("tp") == 2 and pool_size == 8
+    if small:
+        all_old = exchange_old(old_rows)
+    else:
+        all_old = lax.all_gather(old_rows, "pool", axis=0, tiled=False)
 
     chunks = 4
     rows = x_pre.shape[0] // chunks
@@ -383,7 +411,7 @@
             scaling,
         )
     )
-    if lax.axis_size("tp") == 2 and pool_size == 8:
+    if small:
         return gather_out(fresh_rows, all_old, n_old, out_weight)
     all_fresh = lax.all_gather(fresh_rows, "pool", axis=0, tiled=False)
     partial_out = jnp.dot(

time: 159 us -> 137 us (0.86)
  between operations: 13.9 us -> 0.64 us
  matrix products: 38.9 us -> 29.4 us
  starting transfers between devices: 8.37 us -> 17.2 us
  other arithmetic: 17.8 us -> 10.3 us
  Pallas kernels: 43.6 us -> 45.8 us
  local copies, waits for them, and re-layouts: 11.7 us -> 9.71 us
    all_gather x1 -> x0, waiting for transfers between devices: 17.1 us -> none  [body(): all_old = lax.all_gather(old_rows, 'pool', axis=0, tiled=False)]
    ppermute x0 -> x7, waiting for transfers between devices: none -> 11.7 us  [exchange_old(): lax.ppermute(block, 'pool', [(i, i ^ n) for i in everyone])]
    dot_general x4, matrix products: 24 us -> 14.2 us  [body(): jnp.dot(x_pre[c * rows:(c + 1) * rows], late_weight if c else kv_weight,...]
    ppermute x0 -> x7, starting transfers between devices: none -> 9.18 us  [exchange_old(): lax.ppermute(block, 'pool', [(i, i ^ n) for i in everyone])]
    broadcast_in_dim x1, other arithmetic: 6.5 us -> 0.14 us  [body(): pre_rows.T[None]]
    all_to_all x1, waiting for transfers between devices: 6.9 us -> 11.9 us  [body(): lax.all_to_all(sent, 'pool', split_axis=0, concat_axis=0, tiled=True)]
    pallas_call x1, Pallas kernels: 30.8 us -> 33.1 us  [gather_out(): pl.pallas_call(lambda h, *refs: gather_out_kernel(pool // WIDE, h, refs[:...]
    slice x2 -> x4, local copies, waits for them, and re-layouts: 2.26 us -> 0.01 us  [body(): sent = jnp.concatenate([q_dec[:pool_size], x_dec[:pool_size]], axis=-1)]
  transfers between devices with their start and end apart: 7 -> 13, of which waited for: 2 -> 4; matrix products, arithmetic and copies ran while one was open for 38% -> 17% of each run, Pallas kernels for 8% -> 5%
where the time goes in v4:
time: 137 us
  Pallas kernels  45.8 us (33%)
  matrix products  29.4 us (21%)
  waiting for transfers between devices  23.6 us (17%)
  starting transfers between devices  17.2 us (13%)
  other arithmetic  10.3 us (8%)
  local copies, waits for them, and re-layouts  9.71 us (7%)
    pallas_call x1, Pallas kernels, gather_out(): pl.pallas_call(lambda h, *refs: gather_out_kernel(pool // WIDE, h, refs[:...  33.1 us
    dot_general x4, matrix products, body(): jnp.dot(x_pre[c * rows:(c + 1) * rows], late_weight if c else kv_weight,...  14.2 us
    pallas_call x2, Pallas kernels, attend(): pl.pallas_call(lambda *refs: attend_kernel(width, scaling, *refs), grid_s...  12.6 us
    all_to_all x1, waiting for transfers between devices, body(): lax.all_to_all(sent, 'pool', split_axis=0, concat_axis=0, tiled=True)  11.9 us
    ppermute x7, waiting for transfers between devices, exchange_old(): lax.ppermute(block, 'pool', [(i, i ^ n) for i in everyone])  11.7 us
    ppermute x7, starting transfers between devices, exchange_old(): lax.ppermute(block, 'pool', [(i, i ^ n) for i in everyone])  9.18 us
    dot_general x2, matrix products, lift(): jnp.einsum('rihc,hcv->rihv', combined, up_value, preferred_element_type=j...  7.03 us
    all_to_all x1, starting transfers between devices, body(): lax.all_to_all(sent, 'pool', split_axis=0, concat_axis=0, tiled=True)  6.83 us
  transfers between devices with their start and end apart: 13, of which 4 were waited for; matrix products, arithmetic and copies ran while one was open for 17% of the time, Pallas kernels for 5%

profile of v4, /device:TPU:0, one launch (start us, length us, event | category | flops | bytes accessed | tf_op | source)
XLA Modules:
  0.0 136.6 jit_solution(18267493388826826412)
XLA Ops:
  0.0 5.4 %fusion.12 = f32[384,576]{0,1:T(8,128)S(1)} fusion(bf16[3584,576]{0,1:T(8,128)(2,1)} %param.15, bf16[1536,3584]{1,0:T(8,128)(2,1)} %param.12), kind=kOutput, calls=%fused_computation.12 | convolution fusion | flops 1585446912 | bytes 7766016 | tf_op jit(solution)/shard_map/dot_general | solution.py:380
  5.9 1.3 pad_maximum_fusion.2
  7.2 6.8 %all-to-all-start = ((bf16[8,2,15872]{2,1,0:T(2,128)(2,1)}), bf16[8,2,15872]{2,1,0:T(2,128)(2,1)S(1)}, u32[]{:S(2)}, u32[]{:S(2)}) async-start(bf16[8,2,15872]{2,1,0:T(2,128)(2,1)} %pad_maximum_fusion.2), calls=%async_computation | async-start | bytes 1015808 | tf_op jit(solution)/shard_map/all_to_all | solution.py:332
  15.9 0.9 copy-done.4
  16.9 11.9 %all-to-all-done = bf16[8,2,15872]{2,1,0:T(2,128)(2,1)S(1)} async-done(((bf16[8,2,15872]{2,1,0:T(2,128)(2,1)}), bf16[8,2,15872]{2,1,0:T(2,128)(2,1)S(1)}, u32[]{:S(2)}, u32[]{:S(2)}) %all-to-all-start) | async-done | bytes 507936 | tf_op jit(solution)/shard_map/all_to_all | solution.py:332
  29.1 0.9 pad_maximum_fusion.1
  30.0 1.0 reshape.116
  31.0 1.0 copy-done.8
  32.9 3.4 %fusion.49 = f32[28,576]{1,0:T(8,128)S(1)} fusion(bf16[28,3584]{1,0:T(8,128)(2,1)S(1)} %reshape.118, bf16[3584,576]{0,1:T(8,128)(2,1)} %param.15), kind=kOutput, calls=%fused_computation.65 | convolution fusion | flops 115605504 | bytes 4393984 | tf_op jit(solution)/shard_map/dot_general | solution.py:336
  36.4 4.7 %convert_bitcast_fusion = bf16[14,2,64,512]{3,0,1,2:T(8,128)(2,1)S(1)} fusion(bf16[64,128,512]{2,1,0:T(8,128)(2,1)} %param.17, bf16[14,2,64,128]{3,2,1,0:T(8,128)(2,1)S(1)} %slice-done.2), kind=kOutput, calls=%fused_computation.16 | convolution fusion | flops 235798528 | bytes 10682368 | tf_op jit(solution)/shard_map/rihn,hnc->rihc/dot_general | solution.py:341
  42.1 1.7 %copy-done.2 = bf16[6,384,576]{1,2,0:T(8,128)(2,1)S(1)} copy-done((bf16[6,384,576]{1,2,0:T(8,128)(2,1)S(1)}, bf16[6,384,576]{1,2,0:T(8,128)(2,1)}, u32[]{:S(2)}) %copy-start.2) | copy-done | bytes 2654232
  43.8 5.3 %shard_map.118 = bf16[6,128,512]{2,1,0:T(8,128)(2,1)S(1)} custom-call(s32[6]{0:T(128)S(1)} %broadcast_9_refs_0_.2.refs_0_, s32[6]{0:T(128)S(1)} %copy-done.3, bf16[6,128,576]{2,1,0:T(8,128)(2,1)S(1)} %bitcast.70, bf16[6,16,576]{2,1,0:T(8,128)(2,1)S(1)} %pad.14.refs_3_, bf16[6,576,384]{2,1,0:T(8,128)(2,1)S(1)} %bitcast.72), custom_call_target="tpu_custom_call" | custom-call | flops 679477248 | bytes 4423680 | tf_op jit(solution)/shard_map/pallas_call | solution.py:80
  49.2 5.4 %fusion.35 = bf16[6,2,64,128]{3,0,1,2:T(8,128)(2,1)S(1)} fusion(bf16[64,512,128]{2,1,0:T(8,128)(2,1)} %param.18, bf16[6,2,64,512]{3,2,1,0:T(8,128)(2,1)S(1)} %bitcast.69), kind=kOutput, calls=%fused_computation.26 | convolution fusion | flops 100761600 | bytes 9371648 | tf_op jit(solution)/shard_map/rihc,hcv->rihv/dot_general | solution.py:348
  55.0 0.7 slice-done.9
  55.8 2.3 %fusion.16 = f32[384,576]{0,1:T(8,128)S(1)} fusion(bf16[3584,576]{0,1:T(8,128)(2,1)S(1)} %copy-done.9, bf16[1536,3584]{1,0:T(8,128)(2,1)S(1)} %bitcast.84), kind=kOutput, calls=%fused_computation.18 | convolution fusion | flops 1585446912 | bytes 7766016 | tf_op jit(solution)/shard_map/dot_general | solution.py:380
  58.6 3.3 %fusion.19 = f32[384,576]{0,1:T(8,128)} fusion(bf16[3584,576]{0,1:T(8,128)(2,1)S(1)} %copy-done.9, bf16[1536,3584]{1,0:T(8,128)(2,1)S(1)} %bitcast.84), kind=kOutput, calls=%fused_computation.19 | convolution fusion | flops 1585446912 | bytes 7766016 | tf_op jit(solution)/shard_map/dot_general | solution.py:380
  61.9 0.8 collective-permute-start.6
  62.8 1.0 collective-permute-start.8
  63.7 2.6 %collective-permute-start.10 = (bf16[16,8192]{1,0:T(8,128)(2,1)S(1)}, bf16[16,8192]{1,0:T(8,128)(2,1)S(1)}, u32[]{:S(2)}, u32[]{:S(2)}) collective-permute-start(bf16[16,8192]{1,0:T(8,128)(2,1)S(1)} %pad.15.refs_0_), channel_id=1, source_target_pairs={{0,12},{2,14},{4,8},{6,10},{8,4},{10,6},{12,0},{14,2},{1,13},{3,15... | collective-permute-start | bytes 786440 | tf_op jit(solution)/shard_map/ppermute | solution.py:117
  66.4 3.2 %fusion.22 = f32[384,576]{0,1:T(8,128)} fusion(bf16[3584,576]{0,1:T(8,128)(2,1)S(1)} %copy-done.9, bf16[1536,3584]{1,0:T(8,128)(2,1)S(1)} %bitcast.84), kind=kOutput, calls=%fused_computation.20 | convolution fusion | flops 1585446912 | bytes 7766016 | tf_op jit(solution)/shard_map/dot_general | solution.py:380
  70.6 1.5 %add.77 = f32[384,576]{0,1:T(8,128)S(1)} add(f32[384,576]{0,1:T(8,128)} %copy-done.10, f32[384,576]{0,1:T(8,128)} %copy-done.11) | non-fusion elementwise | flops 221184 | bytes 2654208 | tf_op jit(solution)/shard_map/add | solution.py:26
  72.1 2.4 %collective-permute-done.6.refs_2_ = bf16[16,8192]{1,0:T(8,128)(2,1)S(1)} collective-permute-done((bf16[16,8192]{1,0:T(8,128)(2,1)S(1)}, bf16[16,8192]{1,0:T(8,128)(2,1)S(1)}, u32[]{:S(2)}, u32[]{:S(2)}) %collective-permute-start.6) | collective-permute-done | bytes 262176 | tf_op jit(solution)/shard_map/ppermute | solution.py:117
  74.5 2.0 %collective-permute-start.5 = (bf16[16,8192]{1,0:T(8,128)(2,1)S(1)}, bf16[16,8192]{1,0:T(8,128)(2,1)S(1)}, u32[]{:S(2)}, u32[]{:S(2)}) collective-permute-start(bf16[16,8192]{1,0:T(8,128)(2,1)S(1)} %pad.15.refs_0_), channel_id=1, source_target_pairs={{0,2},{2,0},{4,6},{6,4},{8,10},{10,8},{12,14},{14,12},{1,3},{3,1},... | collective-permute-start | bytes 786440 | tf_op jit(solution)/shard_map/ppermute | solution.py:117
  76.5 7.6 %collective-permute-done.8.refs_4_ = bf16[16,8192]{1,0:T(8,128)(2,1)S(1)} collective-permute-done((bf16[16,8192]{1,0:T(8,128)(2,1)S(1)}, bf16[16,8192]{1,0:T(8,128)(2,1)S(1)}, u32[]{:S(2)}, u32[]{:S(2)}) %collective-permute-start.8) | collective-permute-done | bytes 262176 | tf_op jit(solution)/shard_map/ppermute | solution.py:117
  84.8 1.3 collective-permute-start.9
  86.9 1.5 %add.79 = f32[384,576]{0,1:T(8,128)S(1)} add(f32[384,576]{0,1:T(8,128)} %fusion.19, f32[384,576]{0,1:T(8,128)} %collective-permute-done.3) | non-fusion elementwise | flops 221184 | bytes 2654208 | tf_op jit(solution)/shard_map/add | solution.py:26
  88.6 1.7 %add.81 = f32[384,576]{0,1:T(8,128)S(1)} add(f32[384,576]{0,1:T(8,128)} %fusion.22, f32[384,576]{0,1:T(8,128)} %collective-permute-done.4) | non-fusion elementwise | flops 221184 | bytes 2654208 | tf_op jit(solution)/shard_map/add | solution.py:26
  91.1 7.3 %shard_map.119 = bf16[8,128,512]{2,1,0:T(8,128)(2,1)S(1)} custom-call(s32[8]{0:T(128)S(1)} %get-tuple-element.12.refs_0_, s32[8]{0:T(128)S(1)} %add.72.refs_1_, bf16[8,128,576]{2,1,0:T(8,128)(2,1)S(1)} %bitcast.73, bf16[8,16,576]{2,1,0:T(8,128)(2,1)S(1)} %pad.13.refs_3_, bf16[1,576,1536]{2,1,0:T(8,128)(2,1)S(1)} %maximum_bitcast_fusion.refs_4_), custom_call_target="tpu_custom_call" | custom-call | flops 1207959552 | bytes 4128768 | tf_op jit(solution)/shard_map/pallas_call | solution.py:80
  98.5 1.6 %fusion.32 = bf16[8,2,64,128]{3,0,1,2:T(8,128)(2,1)S(1)} fusion(bf16[64,512,128]{2,1,0:T(8,128)(2,1)S(1)} %bitcast.76, bf16[8,2,64,512]{3,2,1,0:T(8,128)(2,1)S(1)} %bitcast.71), kind=kOutput, calls=%fused_computation.25 | convolution fusion | flops 134348800 | bytes 9699328 | tf_op jit(solution)/shard_map/rihc,hcv->rihv/dot_general | solution.py:348
  100.4 1.7 %collective-permute-done.11.refs_7_ = bf16[16,8192]{1,0:T(8,128)(2,1)S(1)} collective-permute-done((bf16[16,8192]{1,0:T(8,128)(2,1)S(1)}, bf16[16,8192]{1,0:T(8,128)(2,1)S(1)}, u32[]{:S(2)}, u32[]{:S(2)}) %collective-permute-start.11) | collective-permute-done | bytes 262176 | tf_op jit(solution)/shard_map/ppermute | solution.py:117
  102.1 33.1 %shard_map.120 = (f32[8,8,896]{2,1,0:T(8,128)S(1)}, f32[4,16,896]{2,1,0:T(8,128)S(1)}) custom-call(bf16[16,8192]{1,0:T(8,128)(2,1)S(1)} %bitcast.74, bf16[16,8192]{1,0:T(8,128)(2,1)S(1)} %pad.15.refs_0_, bf16[16,8192]{1,0:T(8,128)(2,1)S(1)} %collective-permute-done.5.refs_1_, bf16[16,8192]{1,0:T(8,128)(2,1)S(1)} %collective-permute-done.6.refs_2_, ...), custom_call_target="tpu_custom_call" | custom-call | tf_op jit(solution)/shard_map/pallas_call | solution.py:273
  135.9 0.8 convert_element_type.54
  (113 shorter events, 9.6 us)
Async XLA Ops:
  0.0 14.9 %copy-start = (s32[8,8]{1,0:T(8,128)S(1)}, s32[8,8]{1,0:T(8,128)}, u32[]{:S(2)}) copy-start(s32[8,8]{1,0:T(8,128)} %param.23) | copy-start | bytes 772
  0.0 5.9 %slice-start.5 = ((bf16[14,2,3584]{2,1,0:T(2,128)(2,1)}), bf16[8,2,3584]{2,1,0:T(2,128)(2,1)S(1)}, s32[]{:S(2)}) async-start(bf16[14,2,3584]{2,1,0:T(2,128)(2,1)} %param.13), calls=%async_computation.6 | async-start | bytes 229376 | tf_op jit(solution)/shard_map/slice | solution.py:331
  0.0 5.9 %slice-start.3 = ((bf16[14,2,12288]{2,1,0:T(2,128)(2,1)}), bf16[8,2,12288]{2,1,0:T(2,128)(2,1)S(1)}, s32[]{:S(2)}) async-start(bf16[14,2,12288]{2,1,0:T(2,128)(2,1)} %param.14), calls=%async_computation.4 | async-start | bytes 786432 | tf_op jit(solution)/shard_map/slice | solution.py:331
  5.4 10.3 %copy-start.12 = (f32[512]{0:T(512)S(1)}, f32[512]{0:T(512)}, u32[]{:S(2)}) copy-start(f32[512]{0:T(512)} %param.16) | copy-start | bytes 6148
  5.4 10.4 %collective-permute-start.1 = (f32[384,576]{0,1:T(8,128)S(1)}, f32[384,576]{0,1:T(8,128)S(1)}, u32[]{:S(2)}, u32[]{:S(2)}) collective-permute-start(f32[384,576]{0,1:T(8,128)S(1)} %fusion.12), channel_id=1, source_target_pairs={{0,1},{1,0},{2,3},{3,2},{4,5},{5,4},{6,7},{7,6},{8,9},{9,8},{10,11... | collective-permute-start | bytes 2654216 | tf_op jit(solution)/shard_map/ppermute | solution.py:26
  5.9 23.1 %slice-start.4 = ((bf16[14,2,12288]{2,1,0:T(2,128)(2,1)}), bf16[6,2,12288]{2,1,0:T(2,128)(2,1)S(1)}, s32[]{:S(2)}) async-start(bf16[14,2,12288]{2,1,0:T(2,128)(2,1)} %param.14), calls=%async_computation.5 | async-start | bytes 589824 | tf_op jit(solution)/shard_map/slice | solution.py:338
  7.2 21.6 %all-to-all-start = ((bf16[8,2,15872]{2,1,0:T(2,128)(2,1)}), bf16[8,2,15872]{2,1,0:T(2,128)(2,1)S(1)}, u32[]{:S(2)}, u32[]{:S(2)}) async-start(bf16[8,2,15872]{2,1,0:T(2,128)(2,1)} %pad_maximum_fusion.2), calls=%async_computation | async-start | bytes 1015808 | tf_op jit(solution)/shard_map/all_to_all | solution.py:332
  16.9 15.6 %slice-start.6 = ((bf16[14,2,3584]{2,1,0:T(2,128)(2,1)}), bf16[6,2,3584]{2,1,0:T(2,128)(2,1)S(1)}, s32[]{:S(2)}) async-start(bf16[14,2,3584]{2,1,0:T(2,128)(2,1)} %param.13), calls=%async_computation.7 | async-start | bytes 172032 | tf_op jit(solution)/shard_map/slice | solution.py:335
  32.1 4.3 %slice-start.2 = ((bf16[14,2,64,192]{3,2,1,0:T(8,128)(2,1)}), bf16[14,2,64,128]{3,2,1,0:T(8,128)(2,1)S(1)}, s32[]{:S(2)}) async-start(bf16[14,2,64,192]{3,2,1,0:T(8,128)(2,1)} %copy-done.8), calls=%async_computation.3 | async-start | bytes 917504 | tf_op jit(solution)/shard_map/slice | solution.py:342
  32.4 8.7 %copy-start.6 = (bf16[14,2,64,64]{3,0,1,2:T(8,128)(2,1)}, bf16[14,2,64,64]{3,0,1,2:T(8,128)(2,1)S(1)}, u32[]{:S(2)}) copy-start(bf16[14,2,64,64]{3,0,1,2:T(8,128)(2,1)S(1)} %copy.46) | copy-start | bytes 688132
  36.3 5.4 %collective-permute-start = (f32[28,576]{1,0:T(8,128)S(1)}, f32[28,576]{1,0:T(8,128)S(1)}, u32[]{:S(2)}, u32[]{:S(2)}) collective-permute-start(f32[28,576]{1,0:T(8,128)S(1)} %fusion.49), channel_id=1, source_target_pairs={{0,1},{1,0},{2,3},{3,2},{4,5},{5,4},{6,7},{7,6},{8,9},{9,8},{10,11... | collective-permute-start | bytes 193544 | tf_op jit(solution)/shard_map/ppermute | solution.py:26
  42.1 1.8 %copy-start.2 = (bf16[6,384,576]{1,2,0:T(8,128)(2,1)S(1)}, bf16[6,384,576]{1,2,0:T(8,128)(2,1)}, u32[]{:S(2)}) copy-start(bf16[6,384,576]{1,2,0:T(8,128)(2,1)} %param.20) | copy-start | bytes 7962628
  43.8 11.1 %slice-start.7 = ((s8[11010048]{0:T(1024)(128)(4,1)}), s8[4194304]{0:T(1024)(128)(4,1)S(1)}, s32[]{:S(2)}) async-start(s8[11010048]{0:T(1024)(128)(4,1)} %bitcast.83), calls=%async_computation.8 | async-start | bytes 8388608
  49.2 5.8 %copy-start.9 = (bf16[3584,576]{0,1:T(8,128)(2,1)S(1)}, bf16[3584,576]{0,1:T(8,128)(2,1)}, u32[]{:S(2)}) copy-start(bf16[3584,576]{0,1:T(8,128)(2,1)} %param.15) | copy-start | bytes 12386308
  49.2 5.8 %slice-start.8 = ((s8[11010048]{0:T(1024)(128)(4,1)}), s8[4194304]{0:T(1024)(128)(4,1)S(1)}, s32[]{:S(2)}) async-start(s8[11010048]{0:T(1024)(128)(4,1)} %bitcast.83), calls=%async_computation.9 | async-start | bytes 8388608
  49.2 6.6 %slice-start.9 = ((s8[11010048]{0:T(1024)(128)(4,1)}), s8[2621440]{0:T(1024)(128)(4,1)S(1)}, s32[]{:S(2)}) async-start(s8[11010048]{0:T(1024)(128)(4,1)} %bitcast.83), calls=%async_computation.10 | async-start | bytes 5242880
  58.1 3.8 %copy-start.10 = (f32[384,576]{0,1:T(8,128)}, f32[384,576]{0,1:T(8,128)S(1)}, u32[]{:S(2)}) copy-start(f32[384,576]{0,1:T(8,128)S(1)} %fusion.16) | copy-start | bytes 2654212
  58.1 11.5 %collective-permute-start.2 = (f32[384,576]{0,1:T(8,128)S(1)}, f32[384,576]{0,1:T(8,128)S(1)}, u32[]{:S(2)}, u32[]{:S(2)}) collective-permute-start(f32[384,576]{0,1:T(8,128)S(1)} %fusion.16), channel_id=1, source_target_pairs={{0,1},{1,0},{2,3},{3,2},{4,5},{5,4},{6,7},{7,6},{8,9},{9,8},{10,11... | collective-permute-start | bytes 2654216 | tf_op jit(solution)/shard_map/ppermute | solution.py:26
  61.9 24.2 %collective-permute-start.3 = (f32[384,576]{0,1:T(8,128)}, f32[384,576]{0,1:T(8,128)}, u32[]{:S(2)}, u32[]{:S(2)}) collective-permute-start(f32[384,576]{0,1:T(8,128)} %fusion.19), channel_id=1, source_target_pairs={{0,1},{1,0},{2,3},{3,2},{4,5},{5,4},{6,7},{7,6},{8,9},{9,8},{10,11... | collective-permute-start | bytes 2654216 | tf_op jit(solution)/shard_map/ppermute | solution.py:26
  61.9 7.7 %copy-start.7 = (bf16[14,2,64,64]{3,0,1,2:T(8,128)(2,1)S(1)}, bf16[14,2,64,64]{3,0,1,2:T(8,128)(2,1)}, u32[]{:S(2)}) copy-start(bf16[14,2,64,64]{3,0,1,2:T(8,128)(2,1)} %copy-done.6) | copy-start | bytes 688132
  61.9 12.6 %collective-permute-start.6 = (bf16[16,8192]{1,0:T(8,128)(2,1)S(1)}, bf16[16,8192]{1,0:T(8,128)(2,1)S(1)}, u32[]{:S(2)}, u32[]{:S(2)}) collective-permute-start(bf16[16,8192]{1,0:T(8,128)(2,1)S(1)} %pad.15.refs_0_), channel_id=1, source_target_pairs={{0,4},{2,6},{4,0},{6,2},{8,12},{10,14},{12,8},{14,10},{1,5},{3,7},... | collective-permute-start | bytes 786440 | tf_op jit(solution)/shard_map/ppermute | solution.py:117
  62.8 21.3 %collective-permute-start.8 = (bf16[16,8192]{1,0:T(8,128)(2,1)S(1)}, bf16[16,8192]{1,0:T(8,128)(2,1)S(1)}, u32[]{:S(2)}, u32[]{:S(2)}) collective-permute-start(bf16[16,8192]{1,0:T(8,128)(2,1)S(1)} %pad.15.refs_0_), channel_id=1, source_target_pairs={{0,8},{2,10},{4,12},{6,14},{8,0},{10,2},{12,4},{14,6},{1,9},{3,11}... | collective-permute-start | bytes 786440 | tf_op jit(solution)/shard_map/ppermute | solution.py:117
  63.7 21.1 %collective-permute-start.10 = (bf16[16,8192]{1,0:T(8,128)(2,1)S(1)}, bf16[16,8192]{1,0:T(8,128)(2,1)S(1)}, u32[]{:S(2)}, u32[]{:S(2)}) collective-permute-start(bf16[16,8192]{1,0:T(8,128)(2,1)S(1)} %pad.15.refs_0_), channel_id=1, source_target_pairs={{0,12},{2,14},{4,8},{6,10},{8,4},{10,6},{12,0},{14,2},{1,13},{3,15... | collective-permute-start | bytes 786440 | tf_op jit(solution)/shard_map/ppermute | solution.py:117
  69.6 19.0 %collective-permute-start.4 = (f32[384,576]{0,1:T(8,128)}, f32[384,576]{0,1:T(8,128)}, u32[]{:S(2)}, u32[]{:S(2)}) collective-permute-start(f32[384,576]{0,1:T(8,128)} %fusion.22), channel_id=1, source_target_pairs={{0,1},{1,0},{2,3},{3,2},{4,5},{5,4},{6,7},{7,6},{8,9},{9,8},{10,11... | collective-permute-start | bytes 2654216 | tf_op jit(solution)/shard_map/ppermute | solution.py:26
  72.1 18.3 %copy-start.5 = (f32[384,576]{0,1:T(8,128)S(1)}, f32[384,576]{0,1:T(8,128)}, u32[]{:S(2)}) copy-start(f32[384,576]{0,1:T(8,128)} %copy-done.4) | copy-start | bytes 2654212
  74.5 25.9 %collective-permute-start.5 = (bf16[16,8192]{1,0:T(8,128)(2,1)S(1)}, bf16[16,8192]{1,0:T(8,128)(2,1)S(1)}, u32[]{:S(2)}, u32[]{:S(2)}) collective-permute-start(bf16[16,8192]{1,0:T(8,128)(2,1)S(1)} %pad.15.refs_0_), channel_id=1, source_target_pairs={{0,2},{2,0},{4,6},{6,4},{8,10},{10,8},{12,14},{14,12},{1,3},{3,1},... | collective-permute-start | bytes 786440 | tf_op jit(solution)/shard_map/ppermute | solution.py:117
  84.1 16.3 %collective-permute-start.7 = (bf16[16,8192]{1,0:T(8,128)(2,1)S(1)}, bf16[16,8192]{1,0:T(8,128)(2,1)S(1)}, u32[]{:S(2)}, u32[]{:S(2)}) collective-permute-start(bf16[16,8192]{1,0:T(8,128)(2,1)S(1)} %collective-permute-done.6.refs_2_), channel_id=1, source_target_pairs={{0,2},{2,0},{4,6},{6,4},{8,10},{10,8},{12,14},{14,12},{1,3},{3,1},... | collective-permute-start | bytes 786440 | tf_op jit(solution)/shard_map/ppermute | solution.py:117
  84.8 15.6 %collective-permute-start.9 = (bf16[16,8192]{1,0:T(8,128)(2,1)S(1)}, bf16[16,8192]{1,0:T(8,128)(2,1)S(1)}, u32[]{:S(2)}, u32[]{:S(2)}) collective-permute-start(bf16[16,8192]{1,0:T(8,128)(2,1)S(1)} %collective-permute-done.8.refs_4_), channel_id=1, source_target_pairs={{0,2},{2,0},{4,6},{6,4},{8,10},{10,8},{12,14},{14,12},{1,3},{3,1},... | collective-permute-start | bytes 786440 | tf_op jit(solution)/shard_map/ppermute | solution.py:117
  86.1 16.0 %collective-permute-start.11 = (bf16[16,8192]{1,0:T(8,128)(2,1)S(1)}, bf16[16,8192]{1,0:T(8,128)(2,1)S(1)}, u32[]{:S(2)}, u32[]{:S(2)}) collective-permute-start(bf16[16,8192]{1,0:T(8,128)(2,1)S(1)} %collective-permute-done.10.refs_6_), channel_id=1, source_target_pairs={{0,2},{2,0},{4,6},{6,4},{8,10},{10,8},{12,14},{14,12},{1,3},{3,1},... | collective-permute-start | bytes 786440 | tf_op jit(solution)/shard_map/ppermute | solution.py:117
  88.6 9.8 %slice-start = ((s8[8388608]{0:T(1024)(128)(4,1)}), s8[4194304]{0:T(1024)(128)(4,1)S(1)}, s32[]{:S(2)}) async-start(s8[8388608]{0:T(1024)(128)(4,1)} %bitcast.75), calls=%async_computation.1 | async-start | bytes 8388608
  90.4 8.0 %slice-start.1 = ((s8[8388608]{0:T(1024)(128)(4,1)}), s8[4194304]{0:T(1024)(128)(4,1)S(1)}, s32[]{:S(2)}) async-start(s8[8388608]{0:T(1024)(128)(4,1)} %bitcast.75), calls=%async_computation.2 | async-start | bytes 8388608
  102.1 34.5 %copy-start.1 = (s32[8,8]{1,0:T(8,128)S(1)}, s32[8,8]{1,0:T(8,128)}, u32[]{:S(2)}) copy-start(s32[8,8]{1,0:T(8,128)} %param.23) | copy-start | bytes 772
  (4 other events, 3.7 us)

commit v5 on v4

--- a/solution.py
+++ b/solution.py
@@ -330,6 +330,17 @@
     query_cols = q_dec.shape[-1]
     sent = jnp.concatenate([q_dec[:pool_size], x_dec[:pool_size]], axis=-1)
     arrived = lax.all_to_all(sent, "pool", split_axis=0, concat_axis=0, tiled=True)
+    early_weight, _ = lax.optimization_barrier((kv_weight, sent))
+    chunks = 4
+    rows = x_pre.shape[0] // chunks
+
+    def prefill(c, weight):
+        return jnp.dot(
+            x_pre[c * rows : (c + 1) * rows], weight, preferred_element_type=jnp.float32
+        )
+
+    parts = [prefill(c, early_weight) for c in range(2)]
+    arrived, *parts = lax.optimization_barrier((arrived, *parts))
     fresh_q, fresh_x = arrived[..., :query_cols], arrived[..., query_cols:]
 
     x_rows = jnp.concatenate([fresh_x, x_dec[pool_size:]], axis=0).reshape(-1, model_part)
@@ -370,25 +381,9 @@
     else:
         all_old = lax.all_gather(old_rows, "pool", axis=0, tiled=False)
 
-    chunks = 4
-    rows = x_pre.shape[0] // chunks
     late_weight, _ = lax.optimization_barrier((kv_weight, old_rows))
-    pre_rows = jnp.concatenate(
-        [
-            normalize(
-                tp_sum(
-                    jnp.dot(
-                        x_pre[c * rows : (c + 1) * rows],
-                        late_weight if c else kv_weight,
-                        preferred_element_type=jnp.float32,
-                    )
-                ),
-                kv_gain,
-            )
-            for c in range(chunks)
-        ],
-        axis=0,
-    )
+    parts += [prefill(c, late_weight) for c in range(2, chunks)]
+    pre_rows = jnp.concatenate([normalize(tp_sum(part), kv_gain) for part in parts], axis=0)
 
     my_lengths = lax.dynamic_index_in_dim(prompt_lens, own_pool, 0, keepdims=False)
     my_owners = lax.dynamic_index_in_dim(owners, own_pool, 0, keepdims=False)

time: 137 us -> 135 us (0.985)
  waiting for transfers between devices: 23.6 us -> 14.3 us
  Pallas kernels: 45.8 us -> 48.8 us
  matrix products: 29.4 us -> 32.1 us
    all_to_all x1, waiting for transfers between devices: 11.9 us -> 1.32 us  [body(): lax.all_to_all(sent, 'pool', split_axis=0, concat_axis=0, tiled=True)]
    pallas_call x1, Pallas kernels: 33.1 us -> 36.1 us  [gather_out(): pl.pallas_call(lambda h, *refs: gather_out_kernel(pool // WIDE, h, refs[:...]
    dot_general x4, matrix products: 14.2 us -> 17 us  [prefill(): jnp.dot(x_pre[c * rows:(c + 1) * rows], weight, preferred_element_type=jn...]
    unnamed x40 -> x32, local copies, waits for them, and re-layouts: 5.64 us -> 3.32 us
    slice x4 -> x2, local copies, waits for them, and re-layouts: 0.01 us -> 2.26 us  [body(): sent = jnp.concatenate([q_dec[:pool_size], x_dec[:pool_size]], axis=-1)]
  transfers between devices with their start and end apart: 13 -> 13, of which waited for: 4 -> 4; matrix products, arithmetic and copies ran while one was open for 17% -> 29% of each run, Pallas kernels for 5% -> 9%
where the time goes in v5:
time: 135 us; the launch traced here: 134 us
  Pallas kernels  48.8 us (36%)
  matrix products  32.1 us (24%)
  starting transfers between devices  17.8 us (13%)
  waiting for transfers between devices  14.3 us (11%)
  other arithmetic  10.6 us (8%)
  local copies, waits for them, and re-layouts  9.72 us (7%)
    pallas_call x1, Pallas kernels, gather_out(): pl.pallas_call(lambda h, *refs: gather_out_kernel(pool // WIDE, h, refs[:...  36.1 us
    dot_general x4, matrix products, prefill(): jnp.dot(x_pre[c * rows:(c + 1) * rows], weight, preferred_element_type=jn...  17 us
    ppermute x7, waiting for transfers between devices, exchange_old(): lax.ppermute(block, 'pool', [(i, i ^ n) for i in everyone])  13 us
    pallas_call x2, Pallas kernels, attend(): pl.pallas_call(lambda *refs: attend_kernel(width, scaling, *refs), grid_s...  12.6 us
    ppermute x7, starting transfers between devices, exchange_old(): lax.ppermute(block, 'pool', [(i, i ^ n) for i in everyone])  9.36 us
    all_to_all x1, starting transfers between devices, body(): lax.all_to_all(sent, 'pool', split_axis=0, concat_axis=0, tiled=True)  7.25 us
    dot_general x2, matrix products, lift(): jnp.einsum('rihc,hcv->rihv', combined, up_value, preferred_element_type=j...  7.02 us
    dot_general x1, matrix products, body(): jnp.einsum('rihn,hnc->rihc', q_rows[..., :NOPE], up_key, preferred_elemen...  4.68 us
  transfers between devices with their start and end apart: 13, of which 4 were waited for; matrix products, arithmetic and copies ran while one was open for 29% of the time, Pallas kernels for 9%

profile of v5, /device:TPU:0, one launch (start us, length us, event | category | flops | bytes accessed | tf_op | source)
XLA Modules:
  0.0 134.0 jit_solution(17134895549943854377)
XLA Ops:
  0.0 1.0 slice.74
  1.0 1.3 slice.73
  2.3 1.2 pad_maximum_fusion.2
  3.5 7.3 %all-to-all-start = ((bf16[8,2,15872]{2,1,0:T(2,128)(2,1)}), bf16[8,2,15872]{2,1,0:T(2,128)(2,1)S(1)}, u32[]{:S(2)}, u32[]{:S(2)}) async-start(bf16[8,2,15872]{2,1,0:T(2,128)(2,1)} %pad_maximum_fusion.2), calls=%async_computation | async-start | bytes 1015808 | tf_op jit(solution)/shard_map/all_to_all | solution.py:332
  12.3 5.5 %fusion.16 = f32[384,576]{0,1:T(8,128)S(1)} fusion(bf16[3584,576]{0,1:T(8,128)(2,1)} %param.15, bf16[1536,3584]{1,0:T(8,128)(2,1)} %param.12), kind=kOutput, calls=%fused_computation.18 | convolution fusion | flops 1585446912 | bytes 7766016 | tf_op jit(solution)/shard_map/dot_general | solution.py:338
  18.5 5.0 %fusion.19 = f32[384,576]{0,1:T(8,128)} fusion(bf16[3584,576]{0,1:T(8,128)(2,1)S(1)} %copy-done.4, bf16[1536,3584]{1,0:T(8,128)(2,1)} %param.12), kind=kOutput, calls=%fused_computation.19 | convolution fusion | flops 1585446912 | bytes 7766016 | tf_op jit(solution)/shard_map/dot_general | solution.py:338
  23.6 1.3 all-to-all-done
  25.2 0.9 pad_maximum_fusion.1
  26.1 1.0 reshape.116
  28.1 3.4 %fusion.52 = f32[28,576]{1,0:T(8,128)S(1)} fusion(bf16[28,3584]{1,0:T(8,128)(2,1)S(1)} %reshape.118, bf16[3584,576]{0,1:T(8,128)(2,1)} %param.15), kind=kOutput, calls=%fused_computation.66 | convolution fusion | flops 115605504 | bytes 4393984 | tf_op jit(solution)/shard_map/dot_general | solution.py:347
  31.6 4.7 %convert_bitcast_fusion = bf16[14,2,64,512]{3,0,1,2:T(8,128)(2,1)S(1)} fusion(bf16[64,128,512]{2,1,0:T(8,128)(2,1)} %param.17, bf16[14,2,64,128]{3,2,1,0:T(8,128)(2,1)S(1)} %slice.97), kind=kOutput, calls=%fused_computation.16 | convolution fusion | flops 235798528 | bytes 10682368 | tf_op jit(solution)/shard_map/rihn,hnc->rihc/dot_general | solution.py:352
  38.3 1.7 %copy-done.2 = bf16[6,384,576]{1,2,0:T(8,128)(2,1)S(1)} copy-done((bf16[6,384,576]{1,2,0:T(8,128)(2,1)S(1)}, bf16[6,384,576]{1,2,0:T(8,128)(2,1)}, u32[]{:S(2)}) %copy-start.2) | copy-done | bytes 2654232
  40.1 5.3 %shard_map.118 = bf16[6,128,512]{2,1,0:T(8,128)(2,1)S(1)} custom-call(s32[6]{0:T(128)S(1)} %broadcast_9_refs_0_.2.refs_0_, s32[6]{0:T(128)S(1)} %copy-done.3, bf16[6,128,576]{2,1,0:T(8,128)(2,1)S(1)} %bitcast.72, bf16[6,16,576]{2,1,0:T(8,128)(2,1)S(1)} %pad.14.refs_3_, bf16[6,576,384]{2,1,0:T(8,128)(2,1)S(1)} %bitcast.74), custom_call_target="tpu_custom_call" | custom-call | flops 679477248 | bytes 4423680 | tf_op jit(solution)/shard_map/pallas_call | solution.py:80
  45.5 5.4 %fusion.38 = bf16[6,2,64,128]{3,0,1,2:T(8,128)(2,1)S(1)} fusion(bf16[64,512,128]{2,1,0:T(8,128)(2,1)} %param.18, bf16[6,2,64,512]{3,2,1,0:T(8,128)(2,1)S(1)} %bitcast.71), kind=kOutput, calls=%fused_computation.27 | convolution fusion | flops 100761600 | bytes 9371648 | tf_op jit(solution)/shard_map/rihc,hcv->rihv/dot_general | solution.py:359
  51.3 0.7 slice-done.6
  52.0 3.2 %fusion.22 = f32[384,576]{0,1:T(8,128)} fusion(bf16[3584,576]{0,1:T(8,128)(2,1)S(1)} %copy-done.5, bf16[1536,3584]{1,0:T(8,128)(2,1)S(1)} %bitcast.86), kind=kOutput, calls=%fused_computation.20 | convolution fusion | flops 1585446912 | bytes 7766016 | tf_op jit(solution)/shard_map/dot_general | solution.py:338
  55.7 3.2 %fusion.25 = f32[384,576]{0,1:T(8,128)} fusion(bf16[3584,576]{0,1:T(8,128)(2,1)S(1)} %copy-done.5, bf16[1536,3584]{1,0:T(8,128)(2,1)S(1)} %bitcast.86), kind=kOutput, calls=%fused_computation.21 | convolution fusion | flops 1585446912 | bytes 7766016 | tf_op jit(solution)/shard_map/dot_general | solution.py:338
  58.9 0.8 collective-permute-start.6
  59.7 2.3 %collective-permute-start.8 = (bf16[16,8192]{1,0:T(8,128)(2,1)S(1)}, bf16[16,8192]{1,0:T(8,128)(2,1)S(1)}, u32[]{:S(2)}, u32[]{:S(2)}) collective-permute-start(bf16[16,8192]{1,0:T(8,128)(2,1)S(1)} %pad.15.refs_0_), channel_id=1, source_target_pairs={{0,8},{2,10},{4,12},{6,14},{8,0},{10,2},{12,4},{14,6},{1,9},{3,11}... | collective-permute-start | bytes 786440 | tf_op jit(solution)/shard_map/ppermute | solution.py:117
  62.0 1.4 %collective-permute-start.10 = (bf16[16,8192]{1,0:T(8,128)(2,1)S(1)}, bf16[16,8192]{1,0:T(8,128)(2,1)S(1)}, u32[]{:S(2)}, u32[]{:S(2)}) collective-permute-start(bf16[16,8192]{1,0:T(8,128)(2,1)S(1)} %pad.15.refs_0_), channel_id=1, source_target_pairs={{0,12},{2,14},{4,8},{6,10},{8,4},{10,6},{12,0},{14,2},{1,13},{3,15... | collective-permute-start | bytes 786440 | tf_op jit(solution)/shard_map/ppermute | solution.py:117
  63.4 1.3 add.75
  64.8 1.6 %add.77 = f32[384,576]{0,1:T(8,128)S(1)} add(f32[384,576]{0,1:T(8,128)} %fusion.19, f32[384,576]{0,1:T(8,128)} %collective-permute-done.2) | non-fusion elementwise | flops 221184 | bytes 2654208 | tf_op jit(solution)/shard_map/add | solution.py:26
  66.7 5.5 %collective-permute-done.6.refs_2_ = bf16[16,8192]{1,0:T(8,128)(2,1)S(1)} collective-permute-done((bf16[16,8192]{1,0:T(8,128)(2,1)S(1)}, bf16[16,8192]{1,0:T(8,128)(2,1)S(1)}, u32[]{:S(2)}, u32[]{:S(2)}) %collective-permute-start.6) | collective-permute-done | bytes 262176 | tf_op jit(solution)/shard_map/ppermute | solution.py:117
  72.1 1.5 %collective-permute-start.5 = (bf16[16,8192]{1,0:T(8,128)(2,1)S(1)}, bf16[16,8192]{1,0:T(8,128)(2,1)S(1)}, u32[]{:S(2)}, u32[]{:S(2)}) collective-permute-start(bf16[16,8192]{1,0:T(8,128)(2,1)S(1)} %pad.15.refs_0_), channel_id=1, source_target_pairs={{0,2},{2,0},{4,6},{6,4},{8,10},{10,8},{12,14},{14,12},{1,3},{3,1},... | collective-permute-start | bytes 786440 | tf_op jit(solution)/shard_map/ppermute | solution.py:117
  73.6 7.4 %collective-permute-done.8.refs_4_ = bf16[16,8192]{1,0:T(8,128)(2,1)S(1)} collective-permute-done((bf16[16,8192]{1,0:T(8,128)(2,1)S(1)}, bf16[16,8192]{1,0:T(8,128)(2,1)S(1)}, u32[]{:S(2)}, u32[]{:S(2)}) %collective-permute-start.8) | collective-permute-done | bytes 262176 | tf_op jit(solution)/shard_map/ppermute | solution.py:117
  81.0 1.4 %collective-permute-start.7 = (bf16[16,8192]{1,0:T(8,128)(2,1)S(1)}, bf16[16,8192]{1,0:T(8,128)(2,1)S(1)}, u32[]{:S(2)}, u32[]{:S(2)}) collective-permute-start(bf16[16,8192]{1,0:T(8,128)(2,1)S(1)} %collective-permute-done.6.refs_2_), channel_id=1, source_target_pairs={{0,2},{2,0},{4,6},{6,4},{8,10},{10,8},{12,14},{14,12},{1,3},{3,1},... | collective-permute-start | bytes 786440 | tf_op jit(solution)/shard_map/ppermute | solution.py:117
  83.1 1.4 %collective-permute-start.11 = (bf16[16,8192]{1,0:T(8,128)(2,1)S(1)}, bf16[16,8192]{1,0:T(8,128)(2,1)S(1)}, u32[]{:S(2)}, u32[]{:S(2)}) collective-permute-start(bf16[16,8192]{1,0:T(8,128)(2,1)S(1)} %collective-permute-done.10.refs_6_), channel_id=1, source_target_pairs={{0,2},{2,0},{4,6},{6,4},{8,10},{10,8},{12,14},{14,12},{1,3},{3,1},... | collective-permute-start | bytes 786440 | tf_op jit(solution)/shard_map/ppermute | solution.py:117
  84.5 1.5 %add.79 = f32[384,576]{0,1:T(8,128)S(1)} add(f32[384,576]{0,1:T(8,128)} %fusion.22, f32[384,576]{0,1:T(8,128)} %collective-permute-done.3) | non-fusion elementwise | flops 221184 | bytes 2654208 | tf_op jit(solution)/shard_map/add | solution.py:26
  87.0 7.3 %shard_map.119 = bf16[8,128,512]{2,1,0:T(8,128)(2,1)S(1)} custom-call(s32[8]{0:T(128)S(1)} %get-tuple-element.20.refs_0_, s32[8]{0:T(128)S(1)} %add.72.refs_1_, bf16[8,128,576]{2,1,0:T(8,128)(2,1)S(1)} %bitcast.75, bf16[8,16,576]{2,1,0:T(8,128)(2,1)S(1)} %pad.13.refs_3_, bf16[1,576,1536]{2,1,0:T(8,128)(2,1)S(1)} %maximum_bitcast_fusion.refs_4_), custom_call_target="tpu_custom_call" | custom-call | flops 1207959552 | bytes 4128768 | tf_op jit(solution)/shard_map/pallas_call | solution.py:80
  94.4 1.6 %fusion.35 = bf16[8,2,64,128]{3,0,1,2:T(8,128)(2,1)S(1)} fusion(bf16[64,512,128]{2,1,0:T(8,128)(2,1)S(1)} %bitcast.78, bf16[8,2,64,512]{3,2,1,0:T(8,128)(2,1)S(1)} %bitcast.73), kind=kOutput, calls=%fused_computation.26 | convolution fusion | flops 134348800 | bytes 9699328 | tf_op jit(solution)/shard_map/rihc,hcv->rihv/dot_general | solution.py:359
  96.4 36.1 %shard_map.120 = (f32[8,8,896]{2,1,0:T(8,128)S(1)}, f32[4,16,896]{2,1,0:T(8,128)S(1)}) custom-call(bf16[16,8192]{1,0:T(8,128)(2,1)S(1)} %bitcast.76, bf16[16,8192]{1,0:T(8,128)(2,1)S(1)} %pad.15.refs_0_, bf16[16,8192]{1,0:T(8,128)(2,1)S(1)} %collective-permute-done.5.refs_1_, bf16[16,8192]{1,0:T(8,128)(2,1)S(1)} %collective-permute-done.6.refs_2_, ...), custom_call_target="tpu_custom_call" | custom-call | tf_op jit(solution)/shard_map/pallas_call | solution.py:273
  133.2 0.8 convert_element_type.54
  (102 shorter events, 9.2 us)
Async XLA Ops:
  0.0 17.8 %copy-start = (s32[8,8]{1,0:T(8,128)S(1)}, s32[8,8]{1,0:T(8,128)}, u32[]{:S(2)}) copy-start(s32[8,8]{1,0:T(8,128)} %param.23) | copy-start | bytes 772
  3.5 21.4 %all-to-all-start = ((bf16[8,2,15872]{2,1,0:T(2,128)(2,1)}), bf16[8,2,15872]{2,1,0:T(2,128)(2,1)S(1)}, u32[]{:S(2)}, u32[]{:S(2)}) async-start(bf16[8,2,15872]{2,1,0:T(2,128)(2,1)} %pad_maximum_fusion.2), calls=%async_computation | async-start | bytes 1015808 | tf_op jit(solution)/shard_map/all_to_all | solution.py:332
  12.3 5.6 %copy-start.8 = (f32[512]{0:T(512)S(1)}, f32[512]{0:T(512)}, u32[]{:S(2)}) copy-start(f32[512]{0:T(512)} %param.16) | copy-start | bytes 6148
  12.3 6.2 %copy-start.4 = (bf16[3584,576]{0,1:T(8,128)(2,1)S(1)}, bf16[3584,576]{0,1:T(8,128)(2,1)}, u32[]{:S(2)}) copy-start(bf16[3584,576]{0,1:T(8,128)(2,1)} %param.15) | copy-start | bytes 12386308
  18.5 6.6 %slice-start.2 = ((bf16[14,2,12288]{2,1,0:T(2,128)(2,1)}), bf16[6,2,12288]{2,1,0:T(2,128)(2,1)S(1)}, s32[]{:S(2)}) async-start(bf16[14,2,12288]{2,1,0:T(2,128)(2,1)} %param.14), calls=%async_computation.3 | async-start | bytes 589824 | tf_op jit(solution)/shard_map/slice | solution.py:349
  23.6 4.1 %slice-start.3 = ((bf16[14,2,3584]{2,1,0:T(2,128)(2,1)}), bf16[6,2,3584]{2,1,0:T(2,128)(2,1)S(1)}, s32[]{:S(2)}) async-start(bf16[14,2,3584]{2,1,0:T(2,128)(2,1)} %param.13), calls=%async_computation.4 | async-start | bytes 172032 | tf_op jit(solution)/shard_map/slice | solution.py:346
  31.5 6.5 %collective-permute-start = (f32[28,576]{1,0:T(8,128)S(1)}, f32[28,576]{1,0:T(8,128)S(1)}, u32[]{:S(2)}, u32[]{:S(2)}) collective-permute-start(f32[28,576]{1,0:T(8,128)S(1)} %fusion.52), channel_id=1, source_target_pairs={{0,1},{1,0},{2,3},{3,2},{4,5},{5,4},{6,7},{7,6},{8,9},{9,8},{10,11... | collective-permute-start | bytes 193544 | tf_op jit(solution)/shard_map/ppermute | solution.py:26
  36.8 1.3 copy-start.7
  36.8 1.5 %copy-start.3 = (s32[6]{0:T(128)S(1)}, s32[6]{0:T(128)}, u32[]{:S(2)}) copy-start(s32[6]{0:T(128)} %refs_1_.1) | copy-start | bytes 76
  37.1 24.9 %collective-permute-start.1 = (f32[384,576]{0,1:T(8,128)S(1)}, f32[384,576]{0,1:T(8,128)}, u32[]{:S(2)}, u32[]{:S(2)}) collective-permute-start(f32[384,576]{0,1:T(8,128)S(1)} %fusion.16), channel_id=1, source_target_pairs={{0,1},{1,0},{2,3},{3,2},{4,5},{5,4},{6,7},{7,6},{8,9},{9,8},{10,11... | collective-permute-start | bytes 2654216 | tf_op jit(solution)/shard_map/ppermute | solution.py:26
  37.7 27.1 %collective-permute-start.2 = (f32[384,576]{0,1:T(8,128)}, f32[384,576]{0,1:T(8,128)}, u32[]{:S(2)}, u32[]{:S(2)}) collective-permute-start(f32[384,576]{0,1:T(8,128)} %fusion.19), channel_id=1, source_target_pairs={{0,1},{1,0},{2,3},{3,2},{4,5},{5,4},{6,7},{7,6},{8,9},{9,8},{10,11... | collective-permute-start | bytes 2654216 | tf_op jit(solution)/shard_map/ppermute | solution.py:26
  38.3 1.8 %copy-start.2 = (bf16[6,384,576]{1,2,0:T(8,128)(2,1)S(1)}, bf16[6,384,576]{1,2,0:T(8,128)(2,1)}, u32[]{:S(2)}) copy-start(bf16[6,384,576]{1,2,0:T(8,128)(2,1)} %param.20) | copy-start | bytes 7962628
  40.1 11.1 %slice-start.4 = ((s8[11010048]{0:T(1024)(128)(4,1)}), s8[4194304]{0:T(1024)(128)(4,1)S(1)}, s32[]{:S(2)}) async-start(s8[11010048]{0:T(1024)(128)(4,1)} %bitcast.85), calls=%async_computation.5 | async-start | bytes 8388608
  45.4 5.8 %copy-start.5 = (bf16[3584,576]{0,1:T(8,128)(2,1)S(1)}, bf16[3584,576]{0,1:T(8,128)(2,1)}, u32[]{:S(2)}) copy-start(bf16[3584,576]{0,1:T(8,128)(2,1)} %param.15) | copy-start | bytes 12386308
  45.4 5.8 %slice-start.5 = ((s8[11010048]{0:T(1024)(128)(4,1)}), s8[4194304]{0:T(1024)(128)(4,1)S(1)}, s32[]{:S(2)}) async-start(s8[11010048]{0:T(1024)(128)(4,1)} %bitcast.85), calls=%async_computation.6 | async-start | bytes 8388608
  45.5 6.6 %slice-start.6 = ((s8[11010048]{0:T(1024)(128)(4,1)}), s8[2621440]{0:T(1024)(128)(4,1)S(1)}, s32[]{:S(2)}) async-start(s8[11010048]{0:T(1024)(128)(4,1)} %bitcast.85), calls=%async_computation.7 | async-start | bytes 5242880
  55.3 27.8 %collective-permute-start.3 = (f32[384,576]{0,1:T(8,128)}, f32[384,576]{0,1:T(8,128)}, u32[]{:S(2)}, u32[]{:S(2)}) collective-permute-start(f32[384,576]{0,1:T(8,128)} %fusion.22), channel_id=1, source_target_pairs={{0,1},{1,0},{2,3},{3,2},{4,5},{5,4},{6,7},{7,6},{8,9},{9,8},{10,11... | collective-permute-start | bytes 2654216 | tf_op jit(solution)/shard_map/ppermute | solution.py:26
  58.9 13.2 %collective-permute-start.6 = (bf16[16,8192]{1,0:T(8,128)(2,1)S(1)}, bf16[16,8192]{1,0:T(8,128)(2,1)S(1)}, u32[]{:S(2)}, u32[]{:S(2)}) collective-permute-start(bf16[16,8192]{1,0:T(8,128)(2,1)S(1)} %pad.15.refs_0_), channel_id=1, source_target_pairs={{0,4},{2,6},{4,0},{6,2},{8,12},{10,14},{12,8},{14,10},{1,5},{3,7},... | collective-permute-start | bytes 786440 | tf_op jit(solution)/shard_map/ppermute | solution.py:117
  59.7 21.3 %collective-permute-start.8 = (bf16[16,8192]{1,0:T(8,128)(2,1)S(1)}, bf16[16,8192]{1,0:T(8,128)(2,1)S(1)}, u32[]{:S(2)}, u32[]{:S(2)}) collective-permute-start(bf16[16,8192]{1,0:T(8,128)(2,1)S(1)} %pad.15.refs_0_), channel_id=1, source_target_pairs={{0,8},{2,10},{4,12},{6,14},{8,0},{10,2},{12,4},{14,6},{1,9},{3,11}... | collective-permute-start | bytes 786440 | tf_op jit(solution)/shard_map/ppermute | solution.py:117
  62.0 20.4 %collective-permute-start.10 = (bf16[16,8192]{1,0:T(8,128)(2,1)S(1)}, bf16[16,8192]{1,0:T(8,128)(2,1)S(1)}, u32[]{:S(2)}, u32[]{:S(2)}) collective-permute-start(bf16[16,8192]{1,0:T(8,128)(2,1)S(1)} %pad.15.refs_0_), channel_id=1, source_target_pairs={{0,12},{2,14},{4,8},{6,10},{8,4},{10,6},{12,0},{14,2},{1,13},{3,15... | collective-permute-start | bytes 786440 | tf_op jit(solution)/shard_map/ppermute | solution.py:117
  64.7 21.4 %copy-start.6 = (f32[384,576]{0,1:T(8,128)S(1)}, f32[384,576]{0,1:T(8,128)}, u32[]{:S(2)}) copy-start(f32[384,576]{0,1:T(8,128)} %fusion.25) | copy-start | bytes 2654212
  64.8 21.3 %collective-permute-start.4 = (f32[384,576]{0,1:T(8,128)}, f32[384,576]{0,1:T(8,128)S(1)}, u32[]{:S(2)}, u32[]{:S(2)}) collective-permute-start(f32[384,576]{0,1:T(8,128)} %fusion.25), channel_id=1, source_target_pairs={{0,1},{1,0},{2,3},{3,2},{4,5},{5,4},{6,7},{7,6},{8,9},{9,8},{10,11... | collective-permute-start | bytes 2654216 | tf_op jit(solution)/shard_map/ppermute | solution.py:26
  72.1 24.2 %collective-permute-start.5 = (bf16[16,8192]{1,0:T(8,128)(2,1)S(1)}, bf16[16,8192]{1,0:T(8,128)(2,1)S(1)}, u32[]{:S(2)}, u32[]{:S(2)}) collective-permute-start(bf16[16,8192]{1,0:T(8,128)(2,1)S(1)} %pad.15.refs_0_), channel_id=1, source_target_pairs={{0,2},{2,0},{4,6},{6,4},{8,10},{10,8},{12,14},{14,12},{1,3},{3,1},... | collective-permute-start | bytes 786440 | tf_op jit(solution)/shard_map/ppermute | solution.py:117
  81.0 15.3 %collective-permute-start.7 = (bf16[16,8192]{1,0:T(8,128)(2,1)S(1)}, bf16[16,8192]{1,0:T(8,128)(2,1)S(1)}, u32[]{:S(2)}, u32[]{:S(2)}) collective-permute-start(bf16[16,8192]{1,0:T(8,128)(2,1)S(1)} %collective-permute-done.6.refs_2_), channel_id=1, source_target_pairs={{0,2},{2,0},{4,6},{6,4},{8,10},{10,8},{12,14},{14,12},{1,3},{3,1},... | collective-permute-start | bytes 786440 | tf_op jit(solution)/shard_map/ppermute | solution.py:117
  82.4 13.9 %collective-permute-start.9 = (bf16[16,8192]{1,0:T(8,128)(2,1)S(1)}, bf16[16,8192]{1,0:T(8,128)(2,1)S(1)}, u32[]{:S(2)}, u32[]{:S(2)}) collective-permute-start(bf16[16,8192]{1,0:T(8,128)(2,1)S(1)} %collective-permute-done.8.refs_4_), channel_id=1, source_target_pairs={{0,2},{2,0},{4,6},{6,4},{8,10},{10,8},{12,14},{14,12},{1,3},{3,1},... | collective-permute-start | bytes 786440 | tf_op jit(solution)/shard_map/ppermute | solution.py:117
  83.1 13.3 %collective-permute-start.11 = (bf16[16,8192]{1,0:T(8,128)(2,1)S(1)}, bf16[16,8192]{1,0:T(8,128)(2,1)S(1)}, u32[]{:S(2)}, u32[]{:S(2)}) collective-permute-start(bf16[16,8192]{1,0:T(8,128)(2,1)S(1)} %collective-permute-done.10.refs_6_), channel_id=1, source_target_pairs={{0,2},{2,0},{4,6},{6,4},{8,10},{10,8},{12,14},{14,12},{1,3},{3,1},... | collective-permute-start | bytes 786440 | tf_op jit(solution)/shard_map/ppermute | solution.py:117
  86.1 8.2 %slice-start = ((s8[8388608]{0:T(1024)(128)(4,1)}), s8[4194304]{0:T(1024)(128)(4,1)S(1)}, s32[]{:S(2)}) async-start(s8[8388608]{0:T(1024)(128)(4,1)} %bitcast.77), calls=%async_computation.1 | async-start | bytes 8388608
  86.3 8.0 %slice-start.1 = ((s8[8388608]{0:T(1024)(128)(4,1)}), s8[4194304]{0:T(1024)(128)(4,1)S(1)}, s32[]{:S(2)}) async-start(s8[8388608]{0:T(1024)(128)(4,1)} %bitcast.77), calls=%async_computation.2 | async-start | bytes 8388608
  96.4 37.6 %copy-start.1 = (s32[8,8]{1,0:T(8,128)S(1)}, s32[8,8]{1,0:T(8,128)}, u32[]{:S(2)}) copy-start(s32[8,8]{1,0:T(8,128)} %param.23) | copy-start | bytes 772
